TPU v7x, 32 devices: a whole 2x2x4 slice. The times are simulated.
32 devices in a mesh: dp: 16 (over z, y, x), phase: 2 (over core).
Axes of the slice: x: 2, y: 2, z: 4, core: 2. Of those that a mesh axis runs over, the one named last changes fastest.
Arguments:
- inputs: bfloat16 [2, 32, 256, 512], P('phase', 'dp'), may hold values from -6 to 6
- segments: int32 [32, 2, 256], P('dp'), may hold values from 0 to 3, never falling along the last dimension, each value on 1 to 128 neighbouring positions
- delete_target: int32 [32, 256], P('dp'), may hold values from 0 to 1
- place_target: int32 [32, 256], P('dp'), may hold values from 0 to 255
- token_target: int32 [32, 256], P('dp'), may hold values from 0 to 32767
- token_mask: int32 [32, 256], P('dp'), may hold values 0 or 1
- attention_in: bfloat16 [2, 512, 1536], P('phase'), may hold values from -0.25 to 0.25
- attention_out: bfloat16 [2, 512, 512], P('phase'), may hold values from -1.5 to 1.5
- feedforward_in: bfloat16 [2, 512, 2048], P('phase'), may hold values from -0.25 to 0.25
- feedforward_out: bfloat16 [2, 2048, 512], P('phase'), may hold values from -0.125 to 0.125
- norm_gain: float32 [2, 2, 512], P('phase'), may hold values from 0.5 to 1.5
- norm_bias: float32 [2, 2, 512], P('phase'), may hold values from -1.2 to 1.2
- cross_query: bfloat16 [512, 512], replicated, may hold values from -0.25 to 0.25
- cross_keyvalue: bfloat16 [512, 1024], replicated, may hold values from -0.25 to 0.25
- cross_out: bfloat16 [512, 512], replicated, may hold values from -1.5 to 1.5
- cross_gain: float32 [512], replicated, may hold values from 0.5 to 1.5
- cross_bias: float32 [512], replicated, may hold values from -1.2 to 1.2
- head_delete: bfloat16 [512, 2], replicated, may hold values from -0.25 to 0.25
- head_place: bfloat16 [1024, 256], replicated, may hold values from -0.1875 to 0.1875
- head_token: bfloat16 [512, 32768], replicated, may hold values from -0.25 to 0.25
Outputs:
- grad_inputs: float32 [2, 32, 256, 512], P('phase', 'dp')
- grad_attention_in: float32 [2, 512, 1536], P('phase', 'dp')
- grad_attention_out: float32 [2, 512, 512], P('phase', 'dp')
- grad_feedforward_in: float32 [2, 512, 2048], P('phase', 'dp')
- grad_feedforward_out: float32 [2, 2048, 512], P('phase', 'dp')
- grad_norm_gain: float32 [2, 2, 512], P('phase', None, 'dp')
- grad_norm_bias: float32 [2, 2, 512], P('phase', None, 'dp')
- grad_cross_query: float32 [512, 512], P('dp')
- grad_cross_keyvalue: float32 [512, 1024], P('dp')
- grad_cross_out: float32 [512, 512], P('dp')
- grad_cross_gain: float32 [512], P('dp')
- grad_cross_bias: float32 [512], P('dp')
- grad_head_delete: float32 [512, 2], P('dp')
- grad_head_place: float32 [1024, 256], P('dp')
- grad_head_token: float32 [512, 32768], P(None, 'dp')
All inputs are finite; a program needn't handle non-finite values. No bound on the sum of `token_mask` on one device may be relied on, other than what follows from the above.
Results may differ from a plain program's by a relative error of at most 0.017.
Values may be sent and summed in bfloat16 or wider, within the bound.
A program may use at most 832 MiB of HBM per device.

v0:
```python
from functools import partial

import jax
import jax.numpy as jnp
from jax import lax
from jax.sharding import PartitionSpec as P

HEADS = 8
HEAD = 64


MASKED_SCORE = -1e30
NORM_EPSILON = 1e-05


def swapped(block, axis, bit):
    count = lax.axis_size(axis)
    route = []
    for low in range(count):
        high = low | 1 << bit
        if high != low and high < count:
            route += [(low, high), (high, low)]
    return lax.ppermute(block, axis, route)


def layer_norm(residual, gain_vec, bias_vec):
    average = jnp.mean(residual, axis=-1, keepdims=True)
    centered = residual - average
    variance = jnp.mean(centered * centered, axis=-1, keepdims=True)
    return centered * lax.rsqrt(variance + NORM_EPSILON) * gain_vec + bias_vec


def norm_back(residual, gain_vec, bias_vec, grad_out):
    _, pull = jax.vjp(layer_norm, residual, gain_vec, bias_vec)
    return pull(grad_out)


def product(left, right):
    return jnp.dot(left, right, preferred_element_type=jnp.float32)


def inner_left(left, right):
    return lax.dot_general(
        left, right, (((0,), (0,)), ((), ())), preferred_element_type=jnp.float32
    )


def inner_right(left, right):
    return lax.dot_general(
        left, right, (((1,), (1,)), ((), ())), preferred_element_type=jnp.float32
    )


def pick_row(array_in, index):
    return lax.dynamic_index_in_dim(array_in, index, 0, keepdims=False)


def split_heads(matrix):
    return matrix.reshape(matrix.shape[0], HEADS, HEAD)


def attend_forward(queries, key_part, value_part, allowed):
    length = queries.shape[0]
    scores = jnp.einsum(
        "qhd,khd->hqk",
        split_heads(queries),
        split_heads(key_part),
        preferred_element_type=jnp.float32,
    ) * HEAD ** (-0.5)
    scores = jnp.where(allowed[None], scores, MASKED_SCORE)
    row_max = jnp.max(scores, axis=-1, keepdims=True)
    exp_scores = jnp.exp(scores - row_max)
    summed = jnp.sum(exp_scores, axis=-1, keepdims=True)
    prob_rows = (exp_scores / summed).astype(jnp.bfloat16)
    mixed = jnp.einsum(
        "hqk,khd->qhd", prob_rows, split_heads(value_part), preferred_element_type=jnp.float32
    )
    return (mixed.reshape(length, HEADS * HEAD).astype(jnp.bfloat16), row_max + jnp.log(summed))


def attend_backward(queries, key_part, value_part, allowed, log_totals, grad_mixed):
    length = queries.shape[0]
    query_heads = split_heads(queries)
    key_heads = split_heads(key_part)
    grad_heads = split_heads(grad_mixed)
    scores = jnp.einsum(
        "qhd,khd->hqk", query_heads, key_heads, preferred_element_type=jnp.float32
    ) * HEAD ** (-0.5)
    scores = jnp.where(allowed[None], scores, MASKED_SCORE)
    prob_rows = jnp.exp(scores - log_totals)
    grad_probs = jnp.einsum(
        "qhd,khd->hqk", grad_heads, split_heads(value_part), preferred_element_type=jnp.float32
    )
    grad_values = jnp.einsum(
        "hqk,qhd->khd",
        prob_rows.astype(jnp.bfloat16),
        grad_heads,
        preferred_element_type=jnp.float32,
    )
    grad_scores = prob_rows * (grad_probs - jnp.sum(prob_rows * grad_probs, axis=-1, keepdims=True))
    grad_scores = grad_scores.astype(jnp.bfloat16)
    grad_queries = jnp.einsum(
        "hqk,khd->qhd", grad_scores, key_heads, preferred_element_type=jnp.float32
    ) * HEAD ** (-0.5)
    grad_keys = jnp.einsum(
        "hqk,qhd->khd", grad_scores, query_heads, preferred_element_type=jnp.float32
    ) * HEAD ** (-0.5)
    return (
        grad_queries.reshape(length, HEADS * HEAD),
        grad_keys.reshape(length, HEADS * HEAD),
        grad_values.reshape(length, HEADS * HEAD),
    )


def forward_block(states, own_ids, source_ids, source, own_layer, cross_layer, decoder_side):
    qkv_weight, mix_weight, up_weight, down_weight, gains, biases = own_layer
    length, feature_width = states.shape
    projected = product(states, qkv_weight).astype(jnp.bfloat16)
    allowed = own_ids[:, None] == own_ids[None, :]
    mixed_low, log_totals = attend_forward(
        projected[:, :feature_width],
        projected[:, feature_width : 2 * feature_width],
        projected[:, 2 * feature_width :],
        allowed,
    )
    residual = states.astype(jnp.float32) + product(mixed_low, mix_weight)
    after_self = layer_norm(residual, gains[0], biases[0])

    def with_cross(after_self):
        query_weight, keyvalue_weight, cross_mix, cross_scale, cross_shift = cross_layer
        cross_allowed = own_ids[:, None] == source_ids[None, :]
        cross_queries = product(after_self.astype(jnp.bfloat16), query_weight).astype(jnp.bfloat16)
        cross_keys = product(source, keyvalue_weight).astype(jnp.bfloat16)
        cross_mixed, cross_totals = attend_forward(
            cross_queries,
            cross_keys[:, :feature_width],
            cross_keys[:, feature_width:],
            cross_allowed,
        )
        cross_residual = after_self + product(cross_mixed, cross_mix)
        return (
            layer_norm(cross_residual, cross_scale, cross_shift),
            (cross_queries, cross_keys, cross_mixed, cross_totals, cross_residual),
        )

    def without_cross(after_self):
        empty_saved = (
            jnp.zeros((length, feature_width), jnp.bfloat16),
            jnp.zeros((length, 2 * feature_width), jnp.bfloat16),
            jnp.zeros((length, feature_width), jnp.bfloat16),
            jnp.zeros((HEADS, length, 1), jnp.float32),
            jnp.zeros((length, feature_width), jnp.float32),
        )
        return (after_self, empty_saved)

    middle, cross_saved = lax.cond(decoder_side, with_cross, without_cross, after_self)
    pre_act = product(middle.astype(jnp.bfloat16), up_weight)
    hidden = jax.nn.gelu(pre_act, approximate=True).astype(jnp.bfloat16)
    residual_two = middle + product(hidden, down_weight)
    block_out = layer_norm(residual_two, gains[1], biases[1])
    saved = (
        projected,
        mixed_low,
        log_totals,
        residual,
        after_self,
        cross_saved,
        middle,
        pre_act,
        hidden,
        residual_two,
    )
    return (block_out, saved)


def backward_block(
    states, own_ids, source_ids, source, own_layer, cross_layer, saved, grad_out, decoder_side
):
    qkv_weight, mix_weight, up_weight, down_weight, gains, biases = own_layer
    (
        projected,
        mixed_low,
        log_totals,
        residual,
        after_self,
        cross_saved,
        middle,
        pre_act,
        hidden,
        residual_two,
    ) = saved
    length, feature_width = states.shape
    grad_res_two, grad_gain_one, grad_bias_one = norm_back(
        residual_two, gains[1], biases[1], grad_out
    )
    grad_branch = grad_res_two.astype(jnp.bfloat16)
    grad_down = inner_left(hidden, grad_branch)
    grad_hidden = inner_right(grad_branch, down_weight)
    _, gelu_pull = jax.vjp(partial(jax.nn.gelu, approximate=True), pre_act)
    grad_pre = gelu_pull(grad_hidden)[0].astype(jnp.bfloat16)
    grad_up = inner_left(middle.astype(jnp.bfloat16), grad_pre)
    grad_middle = grad_res_two + inner_right(grad_pre, up_weight)

    def cross_back(grad_middle):
        query_weight, keyvalue_weight, cross_mix, cross_scale, cross_shift = cross_layer
        cross_queries, cross_keys, cross_mixed, cross_totals, cross_residual = cross_saved
        cross_allowed = own_ids[:, None] == source_ids[None, :]
        grad_cres, grad_cscale, grad_cshift = norm_back(
            cross_residual, cross_scale, cross_shift, grad_middle
        )
        grad_cbranch = grad_cres.astype(jnp.bfloat16)
        grad_cmix = inner_left(cross_mixed, grad_cbranch)
        grad_cmixed = inner_right(grad_cbranch, cross_mix).astype(jnp.bfloat16)
        grad_cq, grad_ck, grad_cv = attend_backward(
            cross_queries,
            cross_keys[:, :feature_width],
            cross_keys[:, feature_width:],
            cross_allowed,
            cross_totals,
            grad_cmixed,
        )
        grad_cq = grad_cq.astype(jnp.bfloat16)
        grad_ckv = jnp.concatenate([grad_ck, grad_cv], axis=1).astype(jnp.bfloat16)
        grad_query_weight = inner_left(after_self.astype(jnp.bfloat16), grad_cq)
        grad_keyvalue_weight = inner_left(source, grad_ckv)
        grad_after = grad_cres + inner_right(grad_cq, query_weight)
        grad_source = inner_right(grad_ckv, keyvalue_weight)
        return (
            grad_after,
            grad_source,
            (grad_query_weight, grad_keyvalue_weight, grad_cmix, grad_cscale, grad_cshift),
        )

    def skip_cross(grad_middle):
        empty_grads = (
            jnp.zeros((feature_width, feature_width), jnp.float32),
            jnp.zeros((feature_width, 2 * feature_width), jnp.float32),
            jnp.zeros((feature_width, feature_width), jnp.float32),
            jnp.zeros((feature_width,), jnp.float32),
            jnp.zeros((feature_width,), jnp.float32),
        )
        return (grad_middle, jnp.zeros((length, feature_width), jnp.float32), empty_grads)

    grad_after, grad_source, cross_grads = lax.cond(
        decoder_side, cross_back, skip_cross, grad_middle
    )
    grad_residual, grad_gain_zero, grad_bias_zero = norm_back(
        residual, gains[0], biases[0], grad_after
    )
    grad_mix_out = grad_residual.astype(jnp.bfloat16)
    grad_mix = inner_left(mixed_low, grad_mix_out)
    grad_mixed = inner_right(grad_mix_out, mix_weight).astype(jnp.bfloat16)
    allowed = own_ids[:, None] == own_ids[None, :]
    grad_q, grad_k, grad_v = attend_backward(
        projected[:, :feature_width],
        projected[:, feature_width : 2 * feature_width],
        projected[:, 2 * feature_width :],
        allowed,
        log_totals,
        grad_mixed,
    )
    grad_projected = jnp.concatenate([grad_q, grad_k, grad_v], axis=1).astype(jnp.bfloat16)
    grad_qkv = inner_left(states, grad_projected)
    grad_states = grad_residual + inner_right(grad_projected, qkv_weight)
    layer_grads = (
        grad_qkv,
        grad_mix,
        grad_up,
        grad_down,
        jnp.stack([grad_gain_zero, grad_gain_one]),
        jnp.stack([grad_bias_zero, grad_bias_one]),
    )
    return (grad_states, grad_source, layer_grads, cross_grads)


def softmax_terms(logits, labels, row_weight, loss_scale):
    row_max = jnp.max(logits, axis=-1, keepdims=True)
    exp_scores = jnp.exp(logits - row_max)
    summed = jnp.sum(exp_scores, axis=-1, keepdims=True)
    chosen = lax.broadcasted_iota(jnp.int32, logits.shape, 1) == labels[:, None]
    grad_logits = (exp_scores / summed - chosen.astype(jnp.float32)) * (row_weight * loss_scale)[
        :, None
    ]
    return grad_logits.astype(jnp.bfloat16)


def edit_heads(final_out, target_ids, targets, heads_layer, loss_scale):
    delete_weight, place_weight = heads_layer
    delete_rows, place_rows = targets
    half_width = final_out.shape[1]
    final_low = final_out.astype(jnp.bfloat16)
    pair_rows = jnp.concatenate([final_low[:-1], final_low[1:]], axis=1)
    pair_valid = (target_ids[:-1] == target_ids[1:]).astype(jnp.float32)
    grad_delete_logits = softmax_terms(
        product(final_low, delete_weight),
        delete_rows,
        jnp.ones((final_low.shape[0],), jnp.float32),
        loss_scale,
    )
    grad_place_logits = softmax_terms(
        product(pair_rows, place_weight), place_rows[:-1], pair_valid, loss_scale
    )
    grad_delete_weight = inner_left(final_low, grad_delete_logits)
    grad_place_weight = inner_left(pair_rows, grad_place_logits)
    grad_final = inner_right(grad_delete_logits, delete_weight)
    grad_pairs = inner_right(grad_place_logits, place_weight)
    grad_final = (
        grad_final
        + jnp.pad(grad_pairs[:, :half_width], ((0, 1), (0, 0)))
        + jnp.pad(grad_pairs[:, half_width:], ((1, 0), (0, 0)))
    )
    return (grad_final, (grad_delete_weight, grad_place_weight))


def token_whole(final_out, labels, flags, token_weight, loss_scale):
    final_low = final_out.astype(jnp.bfloat16)
    grad_logits = softmax_terms(
        product(final_low, token_weight), labels, flags.astype(jnp.float32), loss_scale
    )
    return (inner_right(grad_logits, token_weight), inner_left(final_low, grad_logits))


def on_device(
    inputs,
    segments,
    delete_target,
    place_target,
    token_target,
    token_mask,
    attention_in,
    attention_out,
    feedforward_in,
    feedforward_out,
    norm_gain,
    norm_bias,
    cross_query,
    cross_keyvalue,
    cross_out,
    cross_gain,
    cross_bias,
    head_delete,
    head_place,
    head_token,
):
    phase_index = lax.axis_index("phase")
    decoder_side = phase_index == 1
    batches = inputs.shape[1]
    length = inputs.shape[2]
    feature_width = inputs.shape[3]
    dp_count = lax.axis_size("dp")
    loss_scale = float(batches * length * dp_count) ** (-0.5)
    own_layer = (
        attention_in[0],
        attention_out[0],
        feedforward_in[0],
        feedforward_out[0],
        norm_gain[0],
        norm_bias[0],
    )
    cross_layer = (cross_query, cross_keyvalue, cross_out, cross_gain, cross_bias)
    heads_layer = (head_delete, head_place)
    vocab_size = head_token.shape[1]
    token_sum = jnp.zeros((feature_width, vocab_size), jnp.float32)
    own_states = inputs[0]
    own_ids = jnp.where(decoder_side, segments[:, 1], segments[:, 0])
    source_ids = segments[:, 0]
    arrived = jnp.zeros((length, feature_width), jnp.bfloat16)
    grad_inputs = jnp.zeros((batches, length, feature_width), jnp.float32)
    layer_sums = tuple((jnp.zeros(weight_arr.shape, jnp.float32) for weight_arr in own_layer))
    cross_sums = tuple((jnp.zeros(weight_arr.shape, jnp.float32) for weight_arr in cross_layer))
    head_sums = tuple((jnp.zeros(weight_arr.shape, jnp.float32) for weight_arr in heads_layer))
    history = {}
    for moment in range(batches + 2):
        if moment <= batches:
            ahead_index = jnp.clip(jnp.where(decoder_side, moment - 1, moment), 0, batches - 1)
            block_out, saved_now = forward_block(
                pick_row(own_states, ahead_index),
                pick_row(own_ids, ahead_index),
                pick_row(source_ids, ahead_index),
                arrived,
                own_layer,
                cross_layer,
                decoder_side,
            )
            history[moment] = saved_now
            encoded_low = block_out.astype(jnp.bfloat16)
        if moment >= 1:
            back_index = jnp.clip(jnp.where(decoder_side, moment - 1, moment - 2), 0, batches - 1)
            validity = jnp.where(decoder_side, 1 <= moment <= batches, moment >= 2).astype(
                jnp.float32
            )
            back_states = pick_row(own_states, back_index)
            back_ids = pick_row(own_ids, back_index)
            back_source_ids = pick_row(source_ids, back_index)
            saved = forward_block(
                back_states,
                back_ids,
                back_source_ids,
                arrived,
                own_layer,
                cross_layer,
                decoder_side,
            )[1]
            final_out = layer_norm(saved[-1], own_layer[4][1], own_layer[5][1])
            targets = (pick_row(delete_target, back_index), pick_row(place_target, back_index))
            token_labels = pick_row(token_target, back_index)
            token_flags = pick_row(token_mask, back_index)

            def decoder_top(final_out):
                grad_final, small_grads = edit_heads(
                    final_out, back_ids, targets, heads_layer, loss_scale
                )
                token_rows_grad, token_piece = token_whole(
                    final_out, token_labels, token_flags, head_token, loss_scale
                )
                return (grad_final + token_rows_grad, small_grads, token_piece)

            def encoder_top(final_out):
                empty_heads = tuple(
                    (jnp.zeros(weight_arr.shape, jnp.float32) for weight_arr in heads_layer)
                )
                return (
                    arrived.astype(jnp.float32),
                    empty_heads,
                    jnp.zeros((feature_width, vocab_size), jnp.float32),
                )

            grad_out, head_grads, token_piece = lax.cond(
                decoder_side, decoder_top, encoder_top, final_out
            )
            token_sum = token_sum + validity * token_piece
            grad_states, grad_source, layer_grads, cross_grads = backward_block(
                back_states,
                back_ids,
                back_source_ids,
                arrived,
                own_layer,
                cross_layer,
                saved,
                grad_out,
                decoder_side,
            )
            layer_sums = jax.tree.map(
                lambda running, fresh: running + validity * fresh, layer_sums, layer_grads
            )
            cross_sums = jax.tree.map(
                lambda running, fresh: running + validity * fresh, cross_sums, cross_grads
            )
            head_sums = jax.tree.map(
                lambda running, fresh: running + validity * fresh, head_sums, head_grads
            )
            old_row = pick_row(grad_inputs, back_index)
            grad_inputs = lax.dynamic_update_index_in_dim(
                grad_inputs, old_row + validity * grad_states, back_index, 0
            )
        if moment <= batches:
            if moment >= 1:
                payload = jnp.where(decoder_side, grad_source.astype(jnp.bfloat16), encoded_low)
            else:
                payload = encoded_low
            arrived = swapped(payload, "phase", 0)
    reduced_layer = (
        lax.psum_scatter(layer_sums[0], "dp", scatter_dimension=0, tiled=True),
        lax.psum_scatter(layer_sums[1], "dp", scatter_dimension=0, tiled=True),
        lax.psum_scatter(layer_sums[2], "dp", scatter_dimension=0, tiled=True),
        lax.psum_scatter(layer_sums[3], "dp", scatter_dimension=0, tiled=True),
        lax.psum_scatter(layer_sums[4], "dp", scatter_dimension=1, tiled=True),
        lax.psum_scatter(layer_sums[5], "dp", scatter_dimension=1, tiled=True),
    )
    partial_top = (
        lax.psum_scatter(cross_sums[0], "dp", scatter_dimension=0, tiled=True),
        lax.psum_scatter(cross_sums[1], "dp", scatter_dimension=0, tiled=True),
        lax.psum_scatter(cross_sums[2], "dp", scatter_dimension=0, tiled=True),
        lax.psum_scatter(cross_sums[3], "dp", scatter_dimension=0, tiled=True),
        lax.psum_scatter(cross_sums[4], "dp", scatter_dimension=0, tiled=True),
        lax.psum_scatter(head_sums[0], "dp", scatter_dimension=0, tiled=True),
        lax.psum_scatter(head_sums[1], "dp", scatter_dimension=0, tiled=True),
        lax.psum_scatter(token_sum, "dp", scatter_dimension=1, tiled=True),
    )
    reduced_all = (
        lax.psum(partial_top[0].astype(jnp.bfloat16), "phase").astype(jnp.float32),
        lax.psum(partial_top[1].astype(jnp.bfloat16), "phase").astype(jnp.float32),
        lax.psum(partial_top[2].astype(jnp.bfloat16), "phase").astype(jnp.float32),
        lax.psum(partial_top[3].astype(jnp.bfloat16), "phase").astype(jnp.float32),
        lax.psum(partial_top[4].astype(jnp.bfloat16), "phase").astype(jnp.float32),
        lax.psum(partial_top[5].astype(jnp.bfloat16), "phase").astype(jnp.float32),
        lax.psum(partial_top[6].astype(jnp.bfloat16), "phase").astype(jnp.float32),
        lax.psum(partial_top[7].astype(jnp.bfloat16), "phase").astype(jnp.float32),
    )
    reduced_top = reduced_all[:7]
    grad_token_out = reduced_all[7]
    return (
        grad_inputs[None],
        reduced_layer[0][None],
        reduced_layer[1][None],
        reduced_layer[2][None],
        reduced_layer[3][None],
        reduced_layer[4][None],
        reduced_layer[5][None],
        reduced_top[0],
        reduced_top[1],
        reduced_top[2],
        reduced_top[3],
        reduced_top[4],
        reduced_top[5],
        reduced_top[6],
        grad_token_out,
    )


def solution(mesh):
    return jax.shard_map(
        on_device,
        mesh=mesh,
        in_specs=(
            P("phase", "dp", None, None),
            P("dp", None, None),
            P("dp", None),
            P("dp", None),
            P("dp", None),
            P("dp", None),
            P("phase", None, None),
            P("phase", None, None),
            P("phase", None, None),
            P("phase", None, None),
            P("phase", None, None),
            P("phase", None, None),
            P(),
            P(),
            P(),
            P(),
            P(),
            P(),
            P(),
            P(),
        ),
        out_specs=(
            P("phase", "dp", None, None),
            P("phase", "dp", None),
            P("phase", "dp", None),
            P("phase", "dp", None),
            P("phase", "dp", None),
            P("phase", None, "dp"),
            P("phase", None, "dp"),
            P("dp", None),
            P("dp", None),
            P("dp", None),
            P("dp"),
            P("dp"),
            P("dp", None),
            P("dp", None),
            P(None, "dp"),
        ),
        check_vma=False,
    )
```

profile of v0, /device:TPU:0, one launch (start us, length us, event | category | flops | bytes accessed | tf_op | source)
XLA Modules:
  0.0 3059.8 jit_solution(17725076906164999525)
XLA Ops:
  17.8 4.2 fusion.481
  25.3 13.7 collective-permute-start
  76.3 3.2 fusion.473
  101.4 4.0 fusion.469
  110.8 4.3 fusion.487
  116.9 4.2 conditional.13
  127.9 31.7 %conditional.14 = (f32[256,512]{1,0:T(8,128)}, f32[512,2]{0,1:T(2,128)S(1)}, f32[1024,256]{1,0:T(8,128)}, f32[512,32768]{1,0:T(8,128)}) conditional(s32[]{:T(128)} %convert_element_type.684, bf16[256,512]{1,0:T(8,128)(2,1)S(1)} %collective-permute-done, (f32[256,512]{1,0:T(8,128)S(1)}, f32[256,512]{1,0:T(8,128)S(1)}, f32[256,512]{1,0:T(8,128)S(1)}, ...), branch_computations={%region_24.25_spmd, %region_25.32_spmd} | conditional | flops 26260336640 | bytes 439617760 | solution.py:428
  128.7 21.0 broadcast.1121
  166.7 4.6 conditional.15
  172.6 158.4 %collective-permute-start.1 = (bf16[256,512]{1,0:T(8,128)(2,1)S(1)}, bf16[256,512]{1,0:T(8,128)(2,1)S(1)}, u32[]{:S(2)}, u32[]{:S(2)}) collective-permute-start(bf16[256,512]{1,0:T(8,128)(2,1)S(1)} %fusion.330), channel_id=1, source_target_pairs={{0,1},{1,0},{2,3},{3,2},{4,5},{5,4},{6,7},{7,6},{8,9},{9,8},{10,11... | collective-permute-start | bytes 786440 | tf_op jit(solution)/shard_map/ppermute | solution.py:23
  332.3 4.2 fusion.493
  338.4 4.2 conditional.17
  348.1 33.6 %conditional.18 = (f32[256,512]{1,0:T(8,128)}, f32[512,2]{0,1:T(2,128)S(1)}, f32[1024,256]{1,0:T(8,128)}, f32[512,32768]{1,0:T(8,128)}) conditional(s32[]{:T(128)} %convert_element_type.684, bf16[256,512]{1,0:T(8,128)(2,1)S(1)} %collective-permute-done.1, (f32[256,512]{1,0:T(8,128)S(1)}, f32[256,512]{1,0:T(8,128)S(1)}, f32[256,512]{1,0:T(8,128)S(1)}, ...), branch_computations={%region_70.71_spmd, %region_71.78_spmd} | conditional | flops 26260336640 | bytes 439617760 | solution.py:428
  349.0 21.0 broadcast.1151
  388.8 4.7 conditional.19
  395.5 157.3 %collective-permute-start.2 = (bf16[256,512]{1,0:T(8,128)(2,1)}, bf16[256,512]{1,0:T(8,128)(2,1)S(1)}, u32[]{:S(2)}, u32[]{:S(2)}) collective-permute-start(bf16[256,512]{1,0:T(8,128)(2,1)} %fusion.331), channel_id=1, source_target_pairs={{0,1},{1,0},{2,3},{3,2},{4,5},{5,4},{6,7},{7,6},{8,9},{9,8},{10,11... | collective-permute-start | bytes 786440 | tf_op jit(solution)/shard_map/ppermute | solution.py:23
  554.8 3.5 conditional.21
  559.1 2.6 fusion.178
  564.3 23.1 conditional.22
  565.2 21.0 broadcast.1181
  588.4 3.0 multiply_add_fusion.13
  591.5 3.9 reduce-scatter.31.cloned.1.call-start
  601.9 3.8 conditional.23
  605.7 3.2 multiply_add_fusion.14
  608.9 3.2 multiply_add_fusion.15
  612.2 5.1 multiply_add_fusion.12
  617.4 83.7 %multiply_add_fusion.9 = f32[512,32768]{1,0:T(8,128)} fusion(f32[512,32768]{1,0:T(8,128)} %get-tuple-element.840, f32[512,32768]{1,0:T(8,128)} %get-tuple-element.839, f32[512,32768]{1,0:T(8,128)} %get-tuple-element.838, f32[]{:T(128)S(6)} %convert_element_type.731, f32[]{:T(128)S(6)} %convert_element_type.683), kind=kLoop, calls=%fused_computation.308 | loop fusion | flops 67108864 | bytes 268435456 | tf_op jit(solution)/shard_map/add | solution.py:431
  706.4 3.2 fusion.421
  718.6 42.9 %all-reduce.8 = (bf16[512]{0:T(512)(128)(2,1)S(1)}, bf16[512]{0:T(512)(128)(2,1)S(1)}) all-reduce(f32[512]{0:T(512)S(1)} %multiply_add_fusion.24, f32[512]{0:T(512)S(1)} %multiply_add_fusion.23), channel_id=11, replica_groups=mesh['dp'=16,'phase'=2] {'dp'}, use_global_device_ids=true, to_apply=%region_162.163.clone | all-reduce | flops 1024 | bytes 6144
  762.7 11.1 reduce-scatter.41.cloned.1.call-done
  775.2 75.0 %reduce-scatter.33.cloned.1.call-done = f32[64,256]{1,0:T(8,128)} async-done(((f32[1024,256]{1,0:T(8,128)}), f32[64,256]{1,0:T(8,128)}) %reduce-scatter.33.cloned.1.call-update) | async-done | bytes 65552 | tf_op jit(solution)/shard_map/reduce_scatter | solution.py:477
  851.6 75.0 %reduce-scatter.31.cloned.1.call-done = f32[32,512]{1,0:T(8,128)} async-done(((f32[512,512]{1,0:T(8,128)}), f32[32,512]{1,0:T(8,128)}) %reduce-scatter.31.cloned.1.call-update) | async-done | bytes 65552 | tf_op jit(solution)/shard_map/reduce_scatter | solution.py:473
  928.0 75.6 %reduce-scatter.27.cloned.1.call-done = f32[32,512]{1,0:T(8,128)} async-done(((f32[512,512]{1,0:T(8,128)}), f32[32,512]{1,0:T(8,128)}) %reduce-scatter.27.cloned.1.call-update) | async-done | bytes 65552 | tf_op jit(solution)/shard_map/reduce_scatter | solution.py:471
  1005.1 77.9 %reduce-scatter.29.cloned.1.call-done = f32[32,1024]{1,0:T(8,128)} async-done(((f32[512,1024]{1,0:T(8,128)}), f32[32,1024]{1,0:T(8,128)}) %reduce-scatter.29.cloned.1.call-update) | async-done | bytes 131088 | tf_op jit(solution)/shard_map/reduce_scatter | solution.py:472
  1084.5 1355.4 %reduce-scatter.35.cloned.1.call-done = f32[512,2048]{1,0:T(8,128)} async-done(((f32[512,32768]{1,0:T(8,128)}), f32[512,2048]{1,0:T(8,128)}) %reduce-scatter.35.cloned.1.call-update) | async-done | bytes 4194320 | tf_op jit(solution)/shard_map/reduce_scatter | solution.py:478
  2440.0 4.0 convert_element_type.769
  2469.6 2.7 fusion.413
  2474.0 3.5 multiply_add_fusion.10
  2482.0 2.9 multiply_add_fusion.11
  2491.0 33.1 %reduce-scatter.39.cloned.1.call-done = f32[32,2]{1,0:T(8,128)} async-done(((f32[512,2]{1,0:T(8,128)}), f32[32,2]{1,0:T(8,128)}) %reduce-scatter.39.cloned.1.call-update) | async-done | bytes 272
  2525.4 73.4 %reduce-scatter.37.cloned.1.call-done = f32[32,2]{1,0:T(8,128)} async-done(((f32[512,2]{1,0:T(8,128)}), f32[32,2]{1,0:T(8,128)}) %reduce-scatter.37.cloned.1.call-update) | async-done | bytes 272
  2600.2 17.4 all-reduce.14.cloned.1.call-done
  2625.1 18.1 all-reduce.16.cloned.1.call-done
  2643.2 4.2 convert_element_type.770
  2648.1 77.1 %reduce-scatter.21.cloned.1.call-done = f32[32,512]{1,0:T(8,128)} async-done(((f32[512,512]{1,0:T(8,128)}), f32[32,512]{1,0:T(8,128)}) %reduce-scatter.21.cloned.1.call-update) | async-done | bytes 65552 | tf_op jit(solution)/shard_map/reduce_scatter | solution.py:464
  2725.1 133.0 %reduce-scatter.19.cloned.1.call-done = f32[32,1536]{1,0:T(8,128)} async-done(((f32[512,1536]{1,0:T(8,128)}), f32[32,1536]{1,0:T(8,128)}) %reduce-scatter.19.cloned.1.call-update) | async-done | bytes 196624 | tf_op jit(solution)/shard_map/reduce_scatter | solution.py:463
  2858.1 97.3 %reduce-scatter.25.cloned.1.call-done = f32[128,512]{1,0:T(8,128)} async-done(((f32[2048,512]{1,0:T(8,128)}), f32[128,512]{1,0:T(8,128)}) %reduce-scatter.25.cloned.1.call-update) | async-done | bytes 262160 | tf_op jit(solution)/shard_map/reduce_scatter | solution.py:466
  2955.5 97.6 %reduce-scatter.23.cloned.1.call-done = f32[32,2048]{1,0:T(8,128)} async-done(((f32[512,2048]{1,0:T(8,128)}), f32[32,2048]{1,0:T(8,128)}) %reduce-scatter.23.cloned.1.call-update) | async-done | bytes 262160 | tf_op jit(solution)/shard_map/reduce_scatter | solution.py:465
  (716 shorter events, 225.5 us)
Async XLA Ops:
  7.2 10.6 copy-start
  7.2 766.6 %reduce-scatter.41.cloned.1.call-start = ((), (), s32[]{:S(2)}) async-start(), calls=%async_computation.23 | async-start | bytes 278528
  8.1 102.7 %copy-start.219 = (s32[2,1,256]{2,1,0:T(1,128)}, s32[2,1,256]{2,1,0:T(1,128)S(1)}, u32[]{:S(2)}) copy-start(s32[2,1,256]{2,1,0:T(1,128)S(1)} %get-tuple-element.1193) | copy-start | bytes 6148
  8.7 38.3 %copy-start.209 = (s32[1,1,256]{2,1,0:T(1,128)}, s32[1,1,256]{2,1,0:T(1,128)S(1)}, u32[]{:S(2)}) copy-start(s32[1,1,256]{2,1,0:T(1,128)S(1)} %get-tuple-element.1260) | copy-start | bytes 3076
  8.7 49.7 %copy-start.211 = (s32[1,1,256]{2,1,0:T(1,128)}, s32[1,1,256]{2,1,0:T(1,128)S(1)}, u32[]{:S(2)}) copy-start(s32[1,1,256]{2,1,0:T(1,128)S(1)} %get-tuple-element.1259) | copy-start | bytes 3076
  8.7 86.2 %copy-start.227 = (s32[1,1,256]{2,1,0:T(1,128)}, s32[1,1,256]{2,1,0:T(1,128)S(1)}, u32[]{:S(2)}) copy-start(s32[1,1,256]{2,1,0:T(1,128)S(1)} %get-tuple-element.1261) | copy-start | bytes 3076
  16.3 91.7 %copy-start.205 = (f32[1,1,512]{2,1,0:T(1,128)}, f32[1,1,512]{2,1,0:T(1,128)S(1)}, u32[]{:S(2)}) copy-start(f32[1,1,512]{2,1,0:T(1,128)S(1)} %get-tuple-element.1190) | copy-start | bytes 6148
  16.3 155.0 %copy-start.207 = (f32[1,1,512]{2,1,0:T(1,128)}, f32[1,1,512]{2,1,0:T(1,128)S(1)}, u32[]{:S(2)}) copy-start(f32[1,1,512]{2,1,0:T(1,128)S(1)} %get-tuple-element.1191) | copy-start | bytes 6148
  22.0 19.1 copy-start.4
  22.0 19.1 copy-start.24
  25.3 85.5 %collective-permute-start = (bf16[256,512]{1,0:T(8,128)(2,1)}, bf16[256,512]{1,0:T(8,128)(2,1)S(1)}, u32[]{:S(2)}, u32[]{:S(2)}) collective-permute-start(bf16[256,512]{1,0:T(8,128)(2,1)} %add_convert_fusion.14), channel_id=1, source_target_pairs={{0,1},{1,0},{2,3},{3,2},{4,5},{5,4},{6,7},{7,6},{8,9},{9,8},{10,11... | collective-permute-start | bytes 786440 | tf_op jit(solution)/shard_map/ppermute | solution.py:23
  57.4 50.7 %copy-start.221 = (f32[256]{0:T(256)}, f32[256]{0:T(256)S(1)}, u32[]{:S(2)}) copy-start(f32[256]{0:T(256)S(1)} %broadcast_multiply_fusion.10) | copy-start | bytes 3076
  58.4 8.1 copy-start.241
  58.4 49.7 %copy-start.233 = (f32[256]{0:T(256)}, f32[256]{0:T(256)S(1)}, u32[]{:S(2)}) copy-start(f32[256]{0:T(256)S(1)} %fusion.387) | copy-start | bytes 3076
  68.8 39.2 %copy-start.223 = (f32[256]{0:T(256)}, f32[256]{0:T(256)S(1)}, u32[]{:S(2)}) copy-start(f32[256]{0:T(256)S(1)} %broadcast_multiply_fusion.14) | copy-start | bytes 3076
  69.8 9.6 copy-start.243
  69.9 38.2 %copy-start.235 = (f32[256]{0:T(256)}, f32[256]{0:T(256)S(1)}, u32[]{:S(2)}) copy-start(f32[256]{0:T(256)S(1)} %fusion.385) | copy-start | bytes 3076
  93.4 14.7 copy-start.225
  94.4 13.6 copy-start.237
  110.8 16.3 copy-start.105
  166.7 165.4 %copy-start.220 = (s32[2,1,256]{2,1,0:T(1,128)S(1)}, s32[2,1,256]{2,1,0:T(1,128)}, u32[]{:S(2)}) copy-start(s32[2,1,256]{2,1,0:T(1,128)} %copy-done.219) | copy-start | bytes 6148
  166.7 165.4 %copy-start.228 = (s32[1,1,256]{2,1,0:T(1,128)S(1)}, s32[1,1,256]{2,1,0:T(1,128)}, u32[]{:S(2)}) copy-start(s32[1,1,256]{2,1,0:T(1,128)} %copy-done.227) | copy-start | bytes 3076
  171.3 160.8 %copy-start.255 = (f32[512]{0:T(512)}, f32[512]{0:T(512)S(1)}, u32[]{:S(2)}) copy-start(f32[512]{0:T(512)S(1)} %get-tuple-element.826) | copy-start | bytes 6148
  171.3 160.8 %copy-start.257 = (f32[512]{0:T(512)}, f32[512]{0:T(512)S(1)}, u32[]{:S(2)}) copy-start(f32[512]{0:T(512)S(1)} %get-tuple-element.829) | copy-start | bytes 6148
  172.6 159.5 %collective-permute-start.1 = (bf16[256,512]{1,0:T(8,128)(2,1)S(1)}, bf16[256,512]{1,0:T(8,128)(2,1)S(1)}, u32[]{:S(2)}, u32[]{:S(2)}) collective-permute-start(bf16[256,512]{1,0:T(8,128)(2,1)S(1)} %fusion.330), channel_id=1, source_target_pairs={{0,1},{1,0},{2,3},{3,2},{4,5},{5,4},{6,7},{7,6},{8,9},{9,8},{10,11... | collective-permute-start | bytes 786440 | tf_op jit(solution)/shard_map/ppermute | solution.py:23
  332.1 16.0 copy-start.107
  332.3 6.0 copy-start.212
  388.8 165.3 %copy-start.210 = (s32[1,1,256]{2,1,0:T(1,128)S(1)}, s32[1,1,256]{2,1,0:T(1,128)}, u32[]{:S(2)}) copy-start(s32[1,1,256]{2,1,0:T(1,128)} %copy-done.209) | copy-start | bytes 3076
  388.8 165.3 %copy-start.239 = (s32[1,1,256]{2,1,0:T(1,128)S(1)}, s32[1,1,256]{2,1,0:T(1,128)}, u32[]{:S(2)}) copy-start(s32[1,1,256]{2,1,0:T(1,128)} %get-tuple-element.1205) | copy-start | bytes 3076
  393.5 161.3 %copy-start.259 = (f32[512]{0:T(512)}, f32[512]{0:T(512)S(1)}, u32[]{:S(2)}) copy-start(f32[512]{0:T(512)S(1)} %get-tuple-element.827) | copy-start | bytes 6148
  393.5 161.3 %copy-start.261 = (f32[512]{0:T(512)}, f32[512]{0:T(512)S(1)}, u32[]{:S(2)}) copy-start(f32[512]{0:T(512)S(1)} %get-tuple-element.830) | copy-start | bytes 6148
  395.5 158.6 %collective-permute-start.2 = (bf16[256,512]{1,0:T(8,128)(2,1)}, bf16[256,512]{1,0:T(8,128)(2,1)S(1)}, u32[]{:S(2)}, u32[]{:S(2)}) collective-permute-start(bf16[256,512]{1,0:T(8,128)(2,1)} %fusion.331), channel_id=1, source_target_pairs={{0,1},{1,0},{2,3},{3,2},{4,5},{5,4},{6,7},{7,6},{8,9},{9,8},{10,11... | collective-permute-start | bytes 786440 | tf_op jit(solution)/shard_map/ppermute | solution.py:23
  564.3 23.1 copy-start.230
  564.3 23.1 copy-start.232
  588.3 261.8 %reduce-scatter.33.cloned.1.call-start = ((), (), s32[]{:S(2)}) async-start(), calls=%async_computation.19 | async-start | bytes 1114112 | tf_op jit(solution)/shard_map/reduce_scatter | solution.py:477
  591.5 335.1 %reduce-scatter.31.cloned.1.call-start = ((), (), s32[]{:S(2)}) async-start(), calls=%async_computation.18 | async-start | bytes 1114112 | tf_op jit(solution)/shard_map/reduce_scatter | solution.py:473
  608.9 394.7 %reduce-scatter.27.cloned.1.call-start = ((), (), s32[]{:S(2)}) async-start(), calls=%async_computation.16 | async-start | bytes 1114112 | tf_op jit(solution)/shard_map/reduce_scatter | solution.py:471
  612.2 470.8 %reduce-scatter.29.cloned.1.call-start = ((), (), s32[]{:S(2)}) async-start(), calls=%async_computation.17 | async-start | bytes 2228224 | tf_op jit(solution)/shard_map/reduce_scatter | solution.py:472
  617.3 1822.6 %reduce-scatter.35.cloned.1.call-start = ((), (), s32[]{:S(2)}) async-start(), calls=%async_computation.20 | async-start | bytes 71303168 | tf_op jit(solution)/shard_map/reduce_scatter | solution.py:478
  701.3 1822.8 %reduce-scatter.39.cloned.1.call-start = ((), (), s32[]{:S(2)}) async-start(), calls=%async_computation.22 | async-start | bytes 278528
  716.5 1882.3 %reduce-scatter.37.cloned.1.call-start = ((), (), s32[]{:S(2)}) async-start(), calls=%async_computation.21 | async-start | bytes 278528
  717.5 1900.1 %all-reduce.14.cloned.1.call-start = ((), (), s32[]{:S(2)}) async-start(), calls=%async_computation.24 | async-start | bytes 199680 | tf_op jit(solution)/shard_map/psum | solution.py:481
  1005.1 1638.2 %all-reduce.16.cloned.1.call-start = ((), (), s32[]{:S(2)}) async-start(), calls=%async_computation.25 | async-start | bytes 4325376 | tf_op jit(solution)/shard_map/psum | solution.py:482
  2443.9 281.2 %reduce-scatter.21.cloned.1.call-start = ((), (), s32[]{:S(2)}) async-start(), calls=%async_computation.13 | async-start | bytes 1114112 | tf_op jit(solution)/shard_map/reduce_scatter | solution.py:464
  2457.8 400.3 %reduce-scatter.19.cloned.1.call-start = ((), (), s32[]{:S(2)}) async-start(), calls=%async_computation.12 | async-start | bytes 3342336 | tf_op jit(solution)/shard_map/reduce_scatter | solution.py:463
  2468.6 486.8 %reduce-scatter.25.cloned.1.call-start = ((), (), s32[]{:S(2)}) async-start(), calls=%async_computation.15 | async-start | bytes 4456448 | tf_op jit(solution)/shard_map/reduce_scatter | solution.py:466
  2477.5 575.6 %reduce-scatter.23.cloned.1.call-start = ((), (), s32[]{:S(2)}) async-start(), calls=%async_computation.14 | async-start | bytes 4456448 | tf_op jit(solution)/shard_map/reduce_scatter | solution.py:465
  2491.0 156.4 %copy-start.156 = (f32[1,2,256,512]{3,2,1,0:T(8,128)}, f32[1,2,256,512]{3,2,1,0:T(8,128)S(1)}, u32[]{:S(2)}) copy-start(f32[1,2,256,512]{3,2,1,0:T(8,128)S(1)} %fusion.291) | copy-start | bytes 3145732
  (189 other events, 371.2 us)
Sparse Core Ops, SparseCore 0:
  588.5 185.3 reduce-scatter.40
  776.2 73.8 reduce-scatter.32
  852.4 74.1 reduce-scatter.30
  929.3 74.2 reduce-scatter.26
  1005.7 77.2 reduce-scatter.28
  1085.2 1354.7 reduce-scatter.34
  2442.3 81.7 reduce-scatter.38
  2526.3 72.4 reduce-scatter.36
  2602.9 14.6 all-reduce.13
  2620.5 22.6 all-reduce.15
  2646.1 79.0 reduce-scatter.20
  2731.3 126.7 reduce-scatter.18
  2861.1 94.3 reduce-scatter.24
  2958.3 94.7 reduce-scatter.22
where the time goes:
time: 3070 us; the launch traced here: 3060 us
  waiting for transfers between devices  2220 us (72%)
  starting transfers between devices  334 us (11%)
  local copies, waits for them, and re-layouts  162 us (5%)
  other arithmetic  158 us (5%)
  matrix products  105 us (3%)
  blocking collectives  42.9 us (1%)
    reduce_scatter x1, waiting for transfers between devices, on_device(): lax.psum_scatter(token_sum, 'dp', scatter_dimension=1, tiled=True)  1360 us
    ppermute x3, starting transfers between devices, swapped(): return lax.ppermute(block, axis, route)  329 us
    reduce_scatter x1, waiting for transfers between devices, on_device(): lax.psum_scatter(layer_sums[0], 'dp', scatter_dimension=0, tiled=True)  133 us
    unnamed x17, waiting for transfers between devices  118 us
    reduce_scatter x1, waiting for transfers between devices, on_device(): lax.psum_scatter(layer_sums[2], 'dp', scatter_dimension=0, tiled=True)  97.6 us
    reduce_scatter x1, waiting for transfers between devices, on_device(): lax.psum_scatter(layer_sums[3], 'dp', scatter_dimension=0, tiled=True)  97.3 us
    another operation x41, local copies, waits for them, and re-layouts  88 us
    add x1, other arithmetic, on_device(): token_sum = token_sum + validity * token_piece  83.7 us
  transfers between devices with their start and end apart: 17, of which 16 were waited for; matrix products, arithmetic and copies ran while one was open for 8% of the time, Pallas kernels for 0%

commit v1 on v0

v1 whole, which is shorter than its diff:
```python
from functools import partial

import jax
import jax.numpy as jnp
from jax import lax
from jax.experimental import pallas as pl
from jax.experimental.pallas import tpu as pltpu
from jax.sharding import PartitionSpec as P

HEADS = 8
HEAD = 64
PAIR = 2 * HEAD
MASKED_SCORE = -1e30
NORM_EPSILON = 1e-05
GROUPS = 16
F32 = jnp.float32
BF16 = jnp.bfloat16
MESH = pl.DeviceIdType.MESH
VMEM = pltpu.VMEM
GELU_C = 0.7978845608028654
GELU_A = 0.044715


def mm(left, right):
    return jnp.dot(left, right, preferred_element_type=F32)


def mm_nt(left, right):
    return lax.dot_general(left, right, (((1,), (1,)), ((), ())), preferred_element_type=F32)


def mm_tn(left, right):
    return lax.dot_general(left, right, (((0,), (0,)), ((), ())), preferred_element_type=F32)


def norm_forward(residual, gain, bias):
    centered = residual - jnp.mean(residual, axis=-1, keepdims=True)
    variance = jnp.mean(centered * centered, axis=-1, keepdims=True)
    return centered * lax.rsqrt(variance + NORM_EPSILON) * gain + bias


def norm_back(residual, gain, grad_out):
    centered = residual - jnp.mean(residual, axis=-1, keepdims=True)
    variance = jnp.mean(centered * centered, axis=-1, keepdims=True)
    scale = lax.rsqrt(variance + NORM_EPSILON)
    unit = centered * scale
    grad_unit = grad_out * gain
    grad_gain = jnp.sum(grad_out * unit, axis=0, keepdims=True)
    grad_bias = jnp.sum(grad_out, axis=0, keepdims=True)
    grad_res = scale * (
        grad_unit
        - jnp.mean(grad_unit, axis=-1, keepdims=True)
        - unit * jnp.mean(grad_unit * unit, axis=-1, keepdims=True)
    )
    return grad_res, grad_gain, grad_bias


def gelu_both(pre):
    square = pre * pre
    bent = jnp.tanh(GELU_C * pre * (1.0 + GELU_A * square))
    half = 0.5 * (1.0 + bent)
    slope = half + (0.5 * GELU_C) * pre * (1.0 - bent * bent) * (1.0 + 3.0 * GELU_A * square)
    return pre * half, slope


def attend_forward(queries, keys, values, allowed, out_ref, totals_ref, rows):
    lane = lax.broadcasted_iota(jnp.int32, (1, PAIR), 1)
    for pair in range(HEADS // 2):
        q, k, v = queries(pair), keys(pair), values(pair)
        mixed = None
        for side in range(2):
            own = (lane < HEAD) if side == 0 else (lane >= HEAD)
            scores = mm_nt(k, jnp.where(own, q * HEAD ** (-0.5), 0))
            scores = jnp.where(allowed, scores, MASKED_SCORE)
            top = jnp.max(scores, axis=0, keepdims=True)
            weights = jnp.exp(scores - top)
            summed = jnp.sum(weights, axis=0, keepdims=True)
            probs = (weights * (1.0 / summed)).astype(BF16)
            totals_ref[2 * pair + side : 2 * pair + side + 1, :] = top + jnp.log(summed)
            part = mm_tn(probs, jnp.where(own, v, 0))
            mixed = part if mixed is None else mixed + part
        out_ref[rows, pair * PAIR : (pair + 1) * PAIR] = mixed.astype(BF16)


def attend_backward(
    queries, keys, values, grads, allowed, totals_ref, put_q, put_k, put_v, between=None
):
    lane = lax.broadcasted_iota(jnp.int32, (1, PAIR), 1)
    for pair in range(HEADS // 2):
        q, k, v, da = queries(pair), keys(pair), values(pair), grads(pair)
        grad_q = grad_k = grad_v = None
        for side in range(2):
            own = (lane < HEAD) if side == 0 else (lane >= HEAD)
            q_own = jnp.where(own, q * HEAD ** (-0.5), 0)
            da_own = jnp.where(own, da, 0)
            scores = jnp.where(allowed, mm_nt(k, q_own), MASKED_SCORE)
            probs = jnp.exp(scores - totals_ref[2 * pair + side : 2 * pair + side + 1, :])
            grad_probs = mm_nt(v, da_own)
            part_v = mm(probs.astype(BF16), da_own)
            shared = jnp.sum(probs * grad_probs, axis=0, keepdims=True)
            grad_scores = (probs * (grad_probs - shared)).astype(BF16)
            part_k = mm(grad_scores, q_own)
            part_q = mm_tn(grad_scores, jnp.where(own, k, 0))
            grad_q = part_q if grad_q is None else grad_q + part_q
            grad_k = part_k if grad_k is None else grad_k + part_k
            grad_v = part_v if grad_v is None else grad_v + part_v
        put_q(pair, (grad_q * HEAD ** (-0.5)).astype(BF16))
        put_k(pair, grad_k.astype(BF16))
        put_v(pair, grad_v.astype(BF16))
        if between is not None:
            between(pair)


def column(pair, offset=0):
    return slice(offset + pair * PAIR, offset + (pair + 1) * PAIR)


def put_shards(ref, first, grad):
    height = grad.shape[0] // GROUPS
    width = ref.shape[2]
    for block in range(grad.shape[1] // width):
        piece = grad[:, block * width : (block + 1) * width].astype(BF16)
        ref[:, first + block * height : first + (block + 1) * height, :] = piece.reshape(
            GROUPS, height, width
        )


def self_forward(
    x_ref, ids_ref, ids_row_ref, qkv_w_ref, mix_w_ref, gain_ref, bias_ref,
    qkv_ref, mixed_ref, res_ref, totals_ref, keep_ref, send_ref,
):
    phase = lax.axis_index("phase")
    count, length = ids_ref.shape[0], ids_ref.shape[1]
    width = x_ref.shape[1]
    for part in range(3):
        cols = slice(part * width, (part + 1) * width)
        qkv_ref[:, cols] = mm(x_ref[...], qkv_w_ref[:, cols]).astype(BF16)
    for row in range(count):
        rows = slice(row * length, (row + 1) * length)
        attend_forward(
            lambda pair: qkv_ref[rows, column(pair)],
            lambda pair: qkv_ref[rows, column(pair, width)],
            lambda pair: qkv_ref[rows, column(pair, 2 * width)],
            ids_ref[row] == ids_row_ref[row],
            mixed_ref, totals_ref.at[row], rows,
        )
    for row in range(count):
        rows = slice(row * length, (row + 1) * length)
        residual = x_ref[rows, :].astype(F32) + mm(mixed_ref[rows, :], mix_w_ref[...])
        res_ref[rows, :] = residual
        after = norm_forward(residual, gain_ref[0:1, :], bias_ref[0:1, :])

        @pl.when(phase == row)
        def _():
            keep_ref[...] = after

        @pl.when(phase != row)
        def _():
            send_ref[...] = after


def load_sided(phase, own_refs, other_refs, enc_refs, dec_refs, sems):
    for i, (own, other, enc, dec) in enumerate(zip(own_refs, other_refs, enc_refs, dec_refs)):
        @pl.when(phase == 0)
        def _():
            pltpu.make_async_copy(own, enc, sems.at[0, i]).start()
            pltpu.make_async_copy(other, dec, sems.at[1, i]).start()

        @pl.when(phase != 0)
        def _():
            pltpu.make_async_copy(other, enc, sems.at[0, i]).start()
            pltpu.make_async_copy(own, dec, sems.at[1, i]).start()

    def wait_enc(i):
        pltpu.make_async_copy(own_refs[i], enc_refs[i], sems.at[0, i]).wait()

    def wait_dec(i):
        pltpu.make_async_copy(own_refs[i], dec_refs[i], sems.at[1, i]).wait()

    return wait_enc, wait_dec


def feed_forward(middle, up_ref, down_ref, hidden_ref, slope_ref):
    width = middle.shape[1]
    low = middle.astype(BF16)
    total = middle
    for part in range(up_ref.shape[1] // width):
        cols = slice(part * width, (part + 1) * width)
        hidden, slope = gelu_both(mm(low, up_ref[:, cols]))
        hidden = hidden.astype(BF16)
        hidden_ref[:, cols] = hidden
        slope_ref[:, cols] = slope.astype(BF16)
        total = total + mm(hidden, down_ref[cols, :])
    return total


def feed_back(grad_res, middle_low, up_ref, down_ref, hidden_ref, slope_ref, put_up, put_down):
    width = grad_res.shape[1]
    branch = grad_res.astype(BF16)
    total = grad_res
    for part in range(up_ref.shape[1] // width):
        cols = slice(part * width, (part + 1) * width)
        put_down(part, mm_tn(hidden_ref[:, cols], branch))
        grad_hidden = mm_nt(branch, down_ref[cols, :])
        grad_pre = (grad_hidden * slope_ref[:, cols].astype(F32)).astype(BF16)
        put_up(part, mm_tn(middle_low, grad_pre))
        total = total + mm_nt(grad_pre, up_ref[:, cols])
    return total


def feed_puts(ref, parts):
    width = ref.shape[2]
    rows = width // GROUPS
    per, tall = GROUPS // parts, parts * rows

    def put_up(part, value):
        put_shards(ref, part * rows, value)

    def put_down(part, value):
        ref[part * per : (part + 1) * per, tall : 2 * tall, :] = value.astype(BF16).reshape(
            per, tall, width
        )

    return put_up, put_down


def class_grads(logits, labels, row_weight, valid):
    lane = lax.broadcasted_iota(jnp.int32, logits.shape, 1)
    logits = jnp.where(lane < valid, logits, -jnp.inf) if valid < logits.shape[1] else logits
    top = jnp.max(logits, axis=-1, keepdims=True)
    weights = jnp.exp(logits - top)
    probs = weights * (1.0 / jnp.sum(weights, axis=-1, keepdims=True))
    return (probs - (lane == labels).astype(F32)) * row_weight


def rows_forward(
    scale, keep_ref, recv_ref, ids_e_ref, ids_d_row_ref, targets_ref,
    up_own, up_other, down_own, down_other, norms_ref,
    cq_w_ref, ckv_w_ref, co_w_ref, cgain_ref, cbias_ref, delete_w_ref, place_w_ref,
    after_e_ref, res_e_ref, after_d_ref, ckv_ref, cq_ref, cmixed_ref, cres_ref, ctotals_ref,
    hid_e_ref, slope_e_ref, hid_d_ref, slope_d_ref, res_d_ref, src_ref,
    low_ref, grad_ref, grad_delete_ref, grad_place_ref,
    up_e, down_e, up_d, down_d, sems,
):
    phase = lax.axis_index("phase")
    width = keep_ref.shape[1]
    wait_enc, wait_dec = load_sided(
        phase, (up_own, down_own), (up_other, down_other), (up_e, down_e), (up_d, down_d), sems
    )

    @pl.when(phase == 0)
    def _():
        after_e_ref[...] = keep_ref[...]
        after_d_ref[...] = recv_ref[...]

    @pl.when(phase != 0)
    def _():
        after_e_ref[...] = recv_ref[...]
        after_d_ref[...] = keep_ref[...]

    wait_enc(0)
    wait_enc(1)
    residual = feed_forward(after_e_ref[...], up_e, down_e, hid_e_ref, slope_e_ref)
    res_e_ref[...] = residual
    src = norm_forward(residual, norms_ref[0:1, :], norms_ref[1:2, :]).astype(BF16)
    src_ref[...] = src
    for part in range(2):
        cols = slice(part * width, (part + 1) * width)
        ckv_ref[:, cols] = mm(src, ckv_w_ref[:, cols]).astype(BF16)
    cq_ref[...] = mm(after_d_ref[...].astype(BF16), cq_w_ref[...]).astype(BF16)
    attend_forward(
        lambda pair: cq_ref[:, column(pair)],
        lambda pair: ckv_ref[:, column(pair)],
        lambda pair: ckv_ref[:, column(pair, width)],
        ids_e_ref[...] == ids_d_row_ref[...],
        cmixed_ref, ctotals_ref, slice(None),
    )
    residual = after_d_ref[...] + mm(cmixed_ref[...], co_w_ref[...])
    cres_ref[...] = residual
    middle = norm_forward(residual, cgain_ref[...], cbias_ref[...])
    wait_dec(0)
    wait_dec(1)
    residual = feed_forward(middle, up_d, down_d, hid_d_ref, slope_d_ref)
    res_d_ref[...] = residual
    low = norm_forward(residual, norms_ref[2:3, :], norms_ref[3:4, :]).astype(BF16)
    low_ref[...] = low
    length = low.shape[0]
    targets = targets_ref[...]
    logits = mm(low, delete_w_ref[...])
    grads = class_grads(logits, targets[:, 0:1], scale, 2).astype(BF16)
    grad_delete_ref[...] = mm_tn(grads, low)[:8]
    grad_low = mm_nt(grads, delete_w_ref[...])
    logits = mm(low, place_w_ref[:width, :]) + pltpu.roll(
        mm(low, place_w_ref[width:, :]), length - 1, 0
    )
    weight = targets[:, 2:3].astype(F32) * scale
    grads = class_grads(logits, targets[:, 1:2], weight, logits.shape[1])
    later = pltpu.roll(grads, 1, 0).astype(BF16)
    grads = grads.astype(BF16)
    classes = grads.shape[1]
    for top, part in enumerate((grads, later)):
        part = mm_tn(low, part).astype(BF16).reshape(GROUPS // 2, 2, width // GROUPS, classes)
        at = slice(top * GROUPS // 2, (top + 1) * GROUPS // 2)
        for half in range(2):
            grad_place_ref[at, :, half * classes : (half + 1) * classes] = part[:, half]
    grad_low = grad_low + mm_nt(grads, place_w_ref[:width, :]) + mm_nt(later, place_w_ref[width:, :])
    grad_ref[...] = grad_low


def rows_backward(
    grad_low_ref, grad_token_ref, ids_e_ref, ids_d_row_ref,
    up_own, up_other, down_own, down_other, norms_ref,
    cq_w_ref, ckv_w_ref, co_w_ref, cgain_ref, cbias_ref,
    after_e_ref, res_e_ref, after_d_ref, ckv_ref, cq_ref, cmixed_ref, cres_ref, ctotals_ref,
    hid_e_ref, slope_e_ref, hid_d_ref, slope_d_ref, res_d_ref, src_ref, grad_place_ref,
    keep_ref, send_ref, own_ref, other_ref, cross_ref, vectors_ref,
    up_e, down_e, up_d, down_d, grad_e, grad_d, after_e_grad, after_d_grad, gq_ref, gckv_ref, sems, out_sems,
):
    phase = lax.axis_index("phase")
    width = grad_low_ref.shape[1]
    wait_enc, wait_dec = load_sided(
        phase, (up_own, down_own), (up_other, down_other), (up_e, down_e), (up_d, down_d), sems
    )
    grad_out = grad_low_ref[...] + grad_token_ref[...]
    grad_res, gain_grad, bias_grad = norm_back(res_d_ref[...], norms_ref[2:3, :], grad_out)
    vectors_ref[2:3, :] = gain_grad
    vectors_ref[3:4, :] = bias_grad
    cres = cres_ref[...]
    middle_low = norm_forward(cres, cgain_ref[...], cbias_ref[...]).astype(BF16)
    wait_dec(0)
    wait_dec(1)
    grad_middle = feed_back(grad_res, middle_low, up_d, down_d, hid_d_ref, slope_d_ref, *feed_puts(grad_d, 4))
    move_d = [
        pltpu.make_async_copy(grad_d, own_ref, out_sems.at[0]),
        pltpu.make_async_copy(grad_d, other_ref, out_sems.at[0]),
    ]

    @pl.when(phase == 0)
    def _():
        move_d[1].start()

    @pl.when(phase != 0)
    def _():
        move_d[0].start()

    grad_res, gain_grad, bias_grad = norm_back(cres, cgain_ref[...], grad_middle)
    vectors_ref[4:5, :] = gain_grad
    vectors_ref[5:6, :] = bias_grad
    branch = grad_res.astype(BF16)
    after_low = after_d_ref[...].astype(BF16)
    rows = width // GROUPS
    put_shards(cross_ref, 3 * rows, mm_tn(cmixed_ref[...], branch))
    grad_mixed = mm_nt(branch, co_w_ref[...]).astype(BF16)

    def put_q(pair, value):
        gq_ref[:, column(pair)] = value

    def put_k(pair, value):
        gckv_ref[:, column(pair)] = value

    def put_v(pair, value):
        gckv_ref[:, column(pair, width)] = value

    attend_backward(
        lambda pair: cq_ref[:, column(pair)],
        lambda pair: ckv_ref[:, column(pair)],
        lambda pair: ckv_ref[:, column(pair, width)],
        lambda pair: grad_mixed[:, column(pair)],
        ids_e_ref[...] == ids_d_row_ref[...],
        ctotals_ref, put_q, put_k, put_v,
    )
    grad_q = gq_ref[...]
    grad_kv = gckv_ref[...]
    put_shards(cross_ref, 0, mm_tn(after_low, grad_q))
    put_shards(cross_ref, rows, mm_tn(src_ref[...], grad_kv))
    cross_ref[:, 4 * rows : 5 * rows, :] = grad_place_ref[...]
    after_d_grad[...] = grad_res + mm_nt(grad_q, cq_w_ref[...])
    grad_src = mm_nt(grad_kv, ckv_w_ref[...]).astype(BF16).astype(F32)
    grad_res, gain_grad, bias_grad = norm_back(res_e_ref[...], norms_ref[0:1, :], grad_src)
    vectors_ref[0:1, :] = gain_grad
    vectors_ref[1:2, :] = bias_grad
    vectors_ref[6:8, :] = jnp.zeros((2, width), F32)
    wait_enc(0)
    wait_enc(1)
    after_e_grad[...] = feed_back(
        grad_res, after_e_ref[...].astype(BF16), up_e, down_e, hid_e_ref, slope_e_ref,
        *feed_puts(grad_e, 4),
    )
    move_e = [
        pltpu.make_async_copy(grad_e, own_ref, out_sems.at[1]),
        pltpu.make_async_copy(grad_e, other_ref, out_sems.at[1]),
    ]

    @pl.when(phase == 0)
    def _():
        move_e[0].start()
        keep_ref[...] = after_e_grad[...]
        send_ref[...] = after_d_grad[...]

    @pl.when(phase != 0)
    def _():
        move_e[1].start()
        keep_ref[...] = after_d_grad[...]
        send_ref[...] = after_e_grad[...]

    move_d[0].wait()
    move_e[0].wait()


def self_backward(
    keep_ref, recv_ref, x_ref, ids_ref, ids_row_ref, qkv_w_ref, mix_w_ref, gain_ref,
    qkv_ref, mixed_ref, res_ref, totals_ref,
    grad_x_ref, shards_ref, vectors_ref,
    after_grad, grad_qkv,
):
    phase = lax.axis_index("phase")
    count, length = ids_ref.shape[0], ids_ref.shape[1]
    width = x_ref.shape[1]
    for row in range(count):
        rows = slice(row * length, (row + 1) * length)

        @pl.when(phase == row)
        def _():
            after_grad[rows, :] = keep_ref[...]

        @pl.when(phase != row)
        def _():
            after_grad[rows, :] = recv_ref[...]

    grad_res, gain_grad, bias_grad = norm_back(res_ref[...], gain_ref[0:1, :], after_grad[...])
    vectors_ref[0:1, :] = gain_grad
    vectors_ref[1:2, :] = bias_grad
    vectors_ref[2:8, :] = jnp.zeros((6, width), F32)
    grad_x_ref[...] = grad_res
    branch = grad_res.astype(BF16)
    rows_each = width // GROUPS
    put_shards(shards_ref, 3 * rows_each, mm_tn(mixed_ref[...], branch))
    grad_mixed = mm_nt(branch, mix_w_ref[...]).astype(BF16)
    for row in range(count):
        rows = slice(row * length, (row + 1) * length)

        def put(offset):
            def store(pair, value):
                grad_qkv[rows, column(pair, offset)] = value

            return store

        attend_backward(
            lambda pair: qkv_ref[rows, column(pair)],
            lambda pair: qkv_ref[rows, column(pair, width)],
            lambda pair: qkv_ref[rows, column(pair, 2 * width)],
            lambda pair: grad_mixed[rows, column(pair)],
            ids_ref[row] == ids_row_ref[row],
            totals_ref.at[row], put(0), put(width), put(2 * width),
        )
    for part in range(3):
        cols = slice(part * width, (part + 1) * width)
        put_shards(shards_ref, part * rows_each, mm_tn(x_ref[...], grad_qkv[:, cols]))
    grad_x_ref[...] += mm_nt(grad_qkv[...], qkv_w_ref[...])


def token_forward(low_ref, weight_ref, probs_ref, totals_ref):
    logits = mm_nt(weight_ref[...], low_ref[...])
    top = jnp.max(logits, axis=0, keepdims=True)
    weights = jnp.exp(logits - top)
    summed = jnp.sum(weights, axis=0, keepdims=True)
    probs_ref[0] = (weights * (1.0 / summed)).astype(BF16)
    totals_ref[0] = top + jnp.log(summed)


def token_backward(
    scale, probs_ref, share_ref, label_ref, low_ref, weight_ref, grad_low_ref, grad_weight_ref, total
):
    step = pl.program_id(0)
    labels = label_ref[0]
    shape = probs_ref.shape[1:]
    offset = (lax.axis_index("dp") * 2 + lax.axis_index("phase")) * shape[0]
    chosen = lax.broadcasted_iota(jnp.int32, shape, 0) == labels - offset
    grads = probs_ref[0].astype(F32) * share_ref[0] - chosen.astype(F32)
    grads = (grads * jnp.where(labels >= 0, scale, 0.0)).astype(BF16)
    grad_low = mm_tn(grads, weight_ref[...]).astype(BF16)
    cap = grad_low_ref.shape[1]
    for block in range(grad_low_ref.shape[0]):
        grad_low_ref[block] = grad_low[block * cap : (block + 1) * cap]
    part = mm(grads, low_ref[...])

    @pl.when(step == 0)
    def _():
        total[...] = part

    @pl.when(step != 0)
    def _():
        total[...] += part

    @pl.when(step == pl.num_programs(0) - 1)
    def _():
        grad_weight_ref[...] = total[...].T


def place_of(dp):
    return lax.rem(dp, 2), lax.rem(dp // 2, 2), dp // 4


def index_of(x, y, z):
    return (z * 2 + y) * 2 + x


def greet(devices):
    barrier = pltpu.get_barrier_semaphore()
    for dp, phase in devices:
        pl.semaphore_signal(barrier, inc=1, device_id=(dp, phase), device_id_type=MESH)
    pl.semaphore_wait(barrier, len(devices))


def remote(src, dst, send, recv, device):
    return pltpu.make_async_remote_copy(
        src_ref=src, dst_ref=dst, send_sem=send, recv_sem=recv, device_id=device, device_id_type=MESH
    )


def gather_kernel(block_ref, out_ref, send, recv, local):
    dp, phase = lax.axis_index("dp"), lax.axis_index("phase")
    x, y, z = place_of(dp)
    x_first = phase == 0
    zs = [lax.rem(z + k, 4) for k in (1, 2, 3)]
    second = index_of(jnp.where(x_first, 1 - x, x), jnp.where(x_first, y, 1 - y), z)
    third = index_of(jnp.where(x_first, x, 1 - x), jnp.where(x_first, 1 - y, y), z)
    greet([(index_of(x, y, k), phase) for k in zs] + [(second, phase), (third, phase), (dp, 1 - phase)])
    own = pltpu.make_async_copy(block_ref, out_ref.at[phase, z, y, x], local.at[0])
    own.start()
    started = []
    first = []
    for k in range(3):
        copy = remote(
            block_ref, out_ref.at[phase, z, y, x], send.at[k], recv.at[k], (index_of(x, y, zs[k]), phase)
        )
        copy.start()
        first.append(copy)
    cross = []

    def to_core(slot, src):
        copy = remote(src, src, send.at[slot], recv.at[slot], (dp, 1 - phase))
        copy.start()
        cross.append(copy)

    mine = remote(block_ref, out_ref.at[phase, z, y, x], send.at[3], recv.at[3], (dp, 1 - phase))
    mine.start()
    cross.append(mine)
    own.wait()
    seconds = []
    x2 = jnp.where(x_first, 1 - x, x)
    y2 = jnp.where(x_first, y, 1 - y)
    x3 = jnp.where(x_first, x, 1 - x)
    y3 = jnp.where(x_first, 1 - y, y)

    def relay(slot, zz, yy, xx, device, into):
        src = out_ref.at[phase, zz, yy, xx]
        copy = remote(src, src, send.at[slot], recv.at[slot], (device, phase))
        copy.start()
        into.append(copy)

    thirds = []
    relay(4, z, y, x, second, seconds)
    relay(8, z, y, x, third, thirds)
    sources = [lax.rem(z + 4 - k, 4) for k in (1, 2, 3)]
    for k in range(3):
        first[k].wait_recv()
        relay(5 + k, sources[k], y, x, second, seconds)
        relay(9 + k, sources[k], y, x, third, thirds)
        to_core(16 + k, out_ref.at[phase, sources[k], y, x])
    order = [z] + sources
    for k in range(4):
        seconds[k].wait_recv()
        relay(12 + k, order[k], y2, x2, third, thirds)
        to_core(19 + k, out_ref.at[phase, order[k], y2, x2])
    for k in range(8):
        thirds_k = thirds[k]
        thirds_k.wait_recv()
        where_y, where_x = (y3, x3) if k < 4 else (1 - y, 1 - x)
        to_core(23 + k, out_ref.at[phase, order[k % 4], where_y, where_x])
    for copy in cross:
        copy.wait_recv()
    for copy in first + seconds + thirds + cross:
        copy.wait_send()


def gather_blocks(block, number):
    dp = lax.axis_size("dp")
    if dp != GROUPS:
        return lax.all_gather(lax.all_gather(block, "dp"), "phase")
    rows, width = block.shape
    out = pl.pallas_call(
        gather_kernel,
        out_shape=jax.ShapeDtypeStruct((2, 4, 2, 2, rows, width), block.dtype),
        in_specs=[pl.BlockSpec(memory_space=pl.ANY)],
        out_specs=pl.BlockSpec(memory_space=pl.ANY),
        scratch_shapes=[
            pltpu.SemaphoreType.DMA((31,)), pltpu.SemaphoreType.DMA((31,)), pltpu.SemaphoreType.DMA((1,)),
        ],
        compiler_params=pltpu.CompilerParams(collective_id=number, has_side_effects=True),
        name="gather_blocks",
    )(block)
    return out.reshape(2, dp, rows, width)


def scatter_kernel(part_ref, out_ref, core_in, third_out, third_in, second_out, second_in, z_out, z_in, send, recv):
    dp, phase = lax.axis_index("dp"), lax.axis_index("phase")
    x, y, z = place_of(dp)
    x_first = phase == 0
    x2 = jnp.where(x_first, 1 - x, x)
    y2 = jnp.where(x_first, y, 1 - y)
    x3 = jnp.where(x_first, x, 1 - x)
    y3 = jnp.where(x_first, 1 - y, y)
    second, third = index_of(x2, y2, z), index_of(x3, y3, z)
    zs = [lax.rem(z + k, 4) for k in (1, 2, 3)]
    greet([(index_of(x, y, k), phase) for k in zs] + [(second, phase), (third, phase), (dp, 1 - phase)])
    order = [lax.rem(z + k, 4) for k in (1, 2, 3, 0)]
    spots = (
        [(zz, 1 - y, 1 - x) for zz in order]
        + [(zz, y3, x3) for zz in order]
        + [(zz, y2, x2) for zz in order]
        + [(zz, y, x) for zz in order]
    )
    theirs = (
        [(zz, 1 - y, 1 - x) for zz in order]
        + [(zz, y2, x2) for zz in order]
        + [(zz, y3, x3) for zz in order]
        + [(zz, y, x) for zz in order]
    )
    cores = []
    for j in range(16):
        zz, yy, xx = theirs[j]
        copy = remote(part_ref.at[1 - phase, zz, yy, xx], core_in.at[j], send.at[j], recv.at[j], (dp, 1 - phase))
        copy.start()
        cores.append(copy)

    def both(j):
        zz, yy, xx = spots[j]
        cores[j].wait_recv()
        return part_ref[phase, zz, yy, xx].astype(F32) + core_in[j].astype(F32)

    thirds = []
    for j in range(8):
        third_out[j] = both(j).astype(BF16)
        copy = remote(third_out.at[j], third_in.at[j], send.at[16 + j], recv.at[16 + j], (third, phase))
        copy.start()
        thirds.append(copy)
    seconds = []
    for j in range(4):
        total = both(8 + j)
        thirds[j].wait_recv()
        second_out[j] = (total + third_in[j].astype(F32)).astype(BF16)
        copy = remote(second_out.at[j], second_in.at[j], send.at[24 + j], recv.at[24 + j], (second, phase))
        copy.start()
        seconds.append(copy)
    along = []
    for j in range(4):
        total = both(12 + j)
        thirds[4 + j].wait_recv()
        total = total + third_in[4 + j].astype(F32)
        seconds[j].wait_recv()
        total = total + second_in[j].astype(F32)
        if j < 3:
            z_out[j] = total.astype(BF16)
            copy = remote(z_out.at[j], z_in.at[j], send.at[28 + j], recv.at[28 + j], (index_of(x, y, zs[j]), phase))
            copy.start()
            along.append(copy)
        else:
            for copy in along:
                copy.wait_recv()
            out_ref[...] = total + z_in[0].astype(F32) + z_in[1].astype(F32) + z_in[2].astype(F32)
    for copy in cores + thirds + seconds + along:
        copy.wait_send()


def scatter_blocks(part, number):
    dp = lax.axis_size("dp")
    if dp != GROUPS:
        part = lax.psum_scatter(part.astype(F32), "phase", scatter_dimension=0, tiled=False)
        return lax.psum_scatter(part, "dp", scatter_dimension=0, tiled=False)
    rows, width = part.shape[2:]
    return pl.pallas_call(
        scatter_kernel,
        out_shape=jax.ShapeDtypeStruct((rows, width), F32),
        in_specs=[pl.BlockSpec(memory_space=VMEM)],
        out_specs=pl.BlockSpec(memory_space=VMEM),
        scratch_shapes=[VMEM((n, rows, width), BF16) for n in (16, 8, 8, 4, 4, 3, 3)]
        + [pltpu.SemaphoreType.DMA((31,)), pltpu.SemaphoreType.DMA((31,))],
        compiler_params=pltpu.CompilerParams(
            collective_id=number, has_side_effects=True, vmem_limit_bytes=48 * 1024 * 1024
        ),
        name="scatter_blocks",
    )(part.reshape(2, 4, 2, 2, rows, width))


def share_kernel(totals_ref, share_ref, near_in, joined, far_in, send, recv):
    dp, phase = lax.axis_index("dp"), lax.axis_index("phase")
    x, y, z = place_of(dp)
    near = [
        (index_of(lax.rem(x + a, 2), lax.rem(y + b, 2), z), lax.rem(phase + c, 2))
        for a in range(2) for b in range(2) for c in range(2) if a + b + c
    ]
    far = [(index_of(x, y, lax.rem(z + k, 4)), phase) for k in (1, 2, 3)]
    greet(near + far)

    def join(parts):
        top = parts[0]
        for part in parts[1:]:
            top = jnp.maximum(top, part)
        summed = jnp.exp(parts[0] - top)
        for part in parts[1:]:
            summed = summed + jnp.exp(part - top)
        return top + jnp.log(summed)

    copies = []
    for j, device in enumerate(near):
        copies.append(remote(totals_ref, near_in.at[j], send.at[j], recv.at[j], device))
        copies[-1].start()
    for copy in copies:
        copy.wait_recv()
    total = join([totals_ref[...]] + [near_in[j] for j in range(7)])
    joined[...] = total
    for j, device in enumerate(far):
        copies.append(remote(joined, far_in.at[j], send.at[7 + j], recv.at[7 + j], device))
        copies[-1].start()
    for copy in copies[7:]:
        copy.wait_recv()
    share_ref[...] = jnp.exp(totals_ref[...] - join([total] + [far_in[j] for j in range(3)]))
    for copy in copies:
        copy.wait_send()


def token_shares(totals, number):
    if lax.axis_size("dp") != GROUPS:
        top = lax.pmax(totals, ("dp", "phase"))
        return jnp.exp(totals - top) / lax.psum(jnp.exp(totals - top), ("dp", "phase"))
    flat = totals.reshape(-1, 128)
    rows = flat.shape[0]
    share = pl.pallas_call(
        share_kernel,
        out_shape=jax.ShapeDtypeStruct((rows, 128), F32),
        in_specs=[pl.BlockSpec(memory_space=VMEM)],
        out_specs=pl.BlockSpec(memory_space=VMEM),
        scratch_shapes=[
            VMEM((7, rows, 128), F32), VMEM((rows, 128), F32), VMEM((3, rows, 128), F32),
            pltpu.SemaphoreType.DMA((10,)), pltpu.SemaphoreType.DMA((10,)),
        ],
        compiler_params=pltpu.CompilerParams(collective_id=number, has_side_effects=True),
        name="token_shares",
    )(flat)
    return share.reshape(totals.shape)


class Exchange:
    def __init__(self, send, recv):
        self.dp, self.phase = lax.axis_index("dp"), lax.axis_index("phase")
        self.x, self.y, self.z = place_of(self.dp)
        x, y, z = self.x, self.y, self.z
        self.along_x, self.along_y = index_of(1 - x, y, z), index_of(x, 1 - y, z)
        self.zs = [lax.rem(z + k, 4) for k in (1, 2, 3)]
        self.send, self.recv, self.used, self.copies = send, recv, 0, []

    def greet(self):
        devices = [(index_of(self.x, self.y, k), self.phase) for k in self.zs]
        greet(devices + [(self.along_x, self.phase), (self.along_y, self.phase), (self.dp, 1 - self.phase)])

    def copy(self, src, dst, device):
        copy = remote(src, dst, self.send.at[self.used], self.recv.at[self.used], device)
        self.used += 1
        copy.start()
        self.copies.append(copy)
        return copy

    def to_core(self, src, dst):
        return self.copy(src, dst, (self.dp, 1 - self.phase))

    def first(self, batch, part):
        start, size, x_first = part
        rows = pl.ds(start, size)
        if x_first:
            src, device = batch.shards.at[:, :, 1 - self.x, rows], self.along_x
        else:
            src, device = batch.shards.at[:, 1 - self.y, :, rows], self.along_y
        return self.copy(src, batch.in1.at[:, :, rows], (device, self.phase))

    def second(self, batch, part):
        start, size, x_first = part
        rows = pl.ds(start, size)
        x, y, in1 = self.x, self.y, batch.in1
        other, device = (1 - y, self.along_y) if x_first else (1 - x, self.along_x)

        def add(i, _):
            zz, which = i // 2, lax.rem(i, 2)
            mine = batch.shards[zz, which, x, rows] if x_first else batch.shards[zz, y, which, rows]
            in1[zz, which, rows] = (in1[zz, which, rows].astype(F32) + mine.astype(F32)).astype(BF16)
            return 0

        lax.fori_loop(0, 8, add, 0)
        return self.copy(in1.at[:, other, rows], batch.in2.at[:, rows], (device, self.phase))

    def third(self, batch, part):
        start, size, x_first = part
        rows = pl.ds(start, size)
        own = self.y if x_first else self.x
        in1, in2 = batch.in1, batch.in2

        def add(zz, _):
            in2[zz, rows] = (in2[zz, rows].astype(F32) + in1[zz, own, rows].astype(F32)).astype(BF16)
            return 0

        lax.fori_loop(0, 4, add, 0)
        return [
            self.copy(in2.at[zz, rows], batch.in3.at[j, rows], (index_of(self.x, self.y, zz), self.phase))
            for j, zz in enumerate(self.zs)
        ]

    def last(self, batch, part, put):
        start, size, _ = part
        rows = pl.ds(start, size)
        in3 = batch.in3
        total = batch.in2[self.z, rows].astype(F32) + in3[0, rows].astype(F32)
        put(rows, total + in3[1, rows].astype(F32) + in3[2, rows].astype(F32))

    def finish(self):
        for copy in self.copies:
            copy.wait_send()


class Batch:
    def __init__(self, exchange, shards, in1, in2, in3, put, parts):
        self.exchange, self.shards, self.in1, self.in2, self.in3 = exchange, shards, in1, in2, in3
        self.put, self.parts = put, parts
        self.waits = [None] * len(parts)

    def from_core(self, copy, own):
        copy.wait_recv()
        shards = self.shards
        for i, part in enumerate(self.parts):
            rows = pl.ds(part[0], part[1])

            def add(j, _):
                at = (j // 4, lax.rem(j // 2, 2), lax.rem(j, 2), rows)
                shards[at] = (shards[at].astype(F32) + own[at].astype(F32)).astype(BF16)
                return 0

            lax.fori_loop(0, GROUPS, add, 0)
            self.waits[i] = self.exchange.first(self, part)

    def start(self):
        for i, part in enumerate(self.parts):
            self.waits[i] = self.exchange.first(self, part)

    def second(self):
        for i, part in enumerate(self.parts):
            self.waits[i].wait_recv()
            self.waits[i] = self.exchange.second(self, part)

    def third(self):
        for i, part in enumerate(self.parts):
            self.waits[i].wait_recv()
            self.waits[i] = self.exchange.third(self, part)

    def last(self):
        for i, part in enumerate(self.parts):
            for copy in self.waits[i]:
                copy.wait_recv()
            self.exchange.last(self, part, self.put)


FF_PARTS = ((0, 64, True), (64, 64, False))
CROSS_PARTS = ((0, 48, False), (48, 32, True))


def backward_kernel(
    grad_low_ref, grad_token_ref, ids_e_ref, ids_d_row_ref,
    up_own, up_other, down_own, down_other, norms_ref,
    cq_w_ref, ckv_w_ref, co_w_ref, cgain_ref, cbias_ref,
    after_e_ref, res_e_ref, after_d_ref, ckv_ref, cq_ref, cmixed_ref, cres_ref, ctotals_ref,
    hid_e_any, slope_e_any, hid_d_any, slope_d_any, res_d_ref, src_ref, grad_place_ref, grad_delete_ref,
    x_ref, ids_ref, ids_row_ref, qkv_w_ref, mix_w_ref, gain_ref,
    qkv_ref, mixed_ref, res_ref, totals_ref,
    grad_x_ref, red_ff_ref, red_attention_ref, red_cross_ref, vectors_ref,
    up, down, hid, slope, grad_d, grad_e, grad_c, grad_a, core_d, core_e, core_c,
    in1_d, in1_e, in1_c, in1_a, in2_d, in2_e, in2_c, in2_a, in3_d, in3_e, in3_c, in3_a,
    after_grads, after_in, gq_ref, gckv_ref, grad_qkv, sums, vec_own, vec_core, vec_1, vec_2, vec_3, vec_in,
    sems, send, recv,
):
    phase = lax.axis_index("phase")
    ex = Exchange(send, recv)
    ex.greet()
    width = grad_low_ref.shape[1]
    each = width // GROUPS
    length = grad_low_ref.shape[0]

    def load(own_side, i):
        hidden, slopes = (hid_e_any, slope_e_any) if own_side == 0 else (hid_d_any, slope_d_any)

        @pl.when(phase == own_side)
        def _():
            pltpu.make_async_copy(up_own, up, sems.at[i]).start()
            pltpu.make_async_copy(down_own, down, sems.at[i + 1]).start()

        @pl.when(phase != own_side)
        def _():
            pltpu.make_async_copy(up_other, up, sems.at[i]).start()
            pltpu.make_async_copy(down_other, down, sems.at[i + 1]).start()

        pltpu.make_async_copy(hidden, hid, sems.at[i + 2]).start()
        pltpu.make_async_copy(slopes, slope, sems.at[i + 3]).start()

    def loaded(i):
        for k, (src, dst) in enumerate(
            ((up_own, up), (down_own, down), (hid_e_any, hid), (slope_e_any, slope))
        ):
            pltpu.make_async_copy(src, dst, sems.at[i + k]).wait()

    def puts(ref):
        def put_up(part, value):
            ref[0, :, :, :, part * each : (part + 1) * each, :] = value.astype(BF16).reshape(
                4, 2, 2, each, width
            )

        def put_down(part, value):
            ref[1, part] = value.astype(BF16).reshape(2, 2, width // 4, width)

        return put_up, put_down

    batch_d = Batch(ex, core_d, in1_d, in2_d, in3_d, None, FF_PARTS)
    batch_e = Batch(ex, core_e, in1_e, in2_e, in3_e, None, FF_PARTS)
    batch_c = Batch(ex, core_c, in1_c, in2_c, in3_c, None, CROSS_PARTS)
    batch_a = Batch(ex, grad_a, in1_a, in2_a, in3_a, None, FF_PARTS)

    load(1, 0)
    grad_out = grad_low_ref[...] + grad_token_ref[...]
    grad_res, gain_grad, bias_grad = norm_back(res_d_ref[...], norms_ref[2:3, :], grad_out)
    vec_own[2:3, :] = gain_grad
    vec_own[3:4, :] = bias_grad
    vec_own[6:8, :] = grad_delete_ref[0:2, :]
    cres = cres_ref[...]
    middle_low = norm_forward(cres, cgain_ref[...], cbias_ref[...]).astype(BF16)
    loaded(0)
    grad_middle = feed_back(grad_res, middle_low, up, down, hid, slope, *puts(grad_d))
    from_d = ex.to_core(grad_d.at[1 - phase], core_d)
    load(0, 4)
    grad_res, gain_grad, bias_grad = norm_back(cres, cgain_ref[...], grad_middle)
    vec_own[4:5, :] = gain_grad
    vec_own[5:6, :] = bias_grad
    branch = grad_res.astype(BF16)

    def put_cross(first, value):
        half_rows = grad_c.shape[4]
        value = value.astype(BF16).reshape(4, 2, 2, each, width)
        for at in range(0, each, 16):
            half, row = divmod(first + at, half_rows)
            grad_c[half, :, :, :, row : row + 16, :] = value[:, :, :, at : at + 16, :]

    put_cross(3 * each, mm_tn(cmixed_ref[...], branch))
    put_cross(4 * each, grad_place_ref[...])
    grad_mixed = mm_nt(branch, co_w_ref[...]).astype(BF16)

    def put_q(pair, value):
        gq_ref[:, column(pair)] = value

    def put_k(pair, value):
        gckv_ref[:, column(pair)] = value

    def put_v(pair, value):
        gckv_ref[:, column(pair, width)] = value

    def between(pair):
        if pair == 2:
            batch_d.from_core(from_d, grad_d.at[phase])

    attend_backward(
        lambda pair: cq_ref[:, column(pair)],
        lambda pair: ckv_ref[:, column(pair)],
        lambda pair: ckv_ref[:, column(pair, width)],
        lambda pair: grad_mixed[:, column(pair)],
        ids_e_ref[...] == ids_d_row_ref[...],
        ctotals_ref, put_q, put_k, put_v, between,
    )
    grad_q = gq_ref[...]
    put_cross(0, mm_tn(after_d_ref[...].astype(BF16), grad_q))
    for part in range(2):
        put_cross((1 + part) * each, mm_tn(src_ref[...], gckv_ref[:, part * width : (part + 1) * width]))
    from_c = ex.to_core(grad_c.at[1 - phase], core_c)
    after_grads[1] = grad_res + mm_nt(grad_q, cq_w_ref[...])
    grad_src = mm_nt(gckv_ref[...], ckv_w_ref[...]).astype(BF16).astype(F32)
    grad_res, gain_grad, bias_grad = norm_back(res_e_ref[...], norms_ref[0:1, :], grad_src)
    vec_own[0:1, :] = gain_grad
    vec_own[1:2, :] = bias_grad
    from_v = ex.to_core(vec_own, vec_core)
    loaded(4)
    after_grads[0] = feed_back(
        grad_res, after_e_ref[...].astype(BF16), up, down, hid, slope, *puts(grad_e)
    )
    from_e = ex.to_core(grad_e.at[1 - phase], core_e)
    from_after = ex.to_core(after_grads.at[1 - phase], after_in)
    batch_c.from_core(from_c, grad_c.at[phase])
    first_vectors = []
    for turn in range(2):
        row = phase if turn == 0 else 1 - phase
        rows = pl.ds(pl.multiple_of(row * length, length), length)
        if turn == 0:
            grad_after = after_grads[phase]
        else:
            from_after.wait_recv()
            grad_after = after_in[...]
        grad_res, gain_grad, bias_grad = norm_back(res_ref[rows, :], gain_ref[0:1, :], grad_after)
        first_vectors.append((gain_grad, bias_grad))
        grad_x_ref[rows, :] = grad_res
        branch = grad_res.astype(BF16)
        if turn == 0:
            first_branch, first_rows = branch, rows
        grad_mixed = mm_nt(branch, mix_w_ref[...]).astype(BF16)

        def put(offset):
            def store(pair, value):
                grad_qkv[rows, column(pair, offset)] = value

            return store

        def between(pair):
            if turn == 0 and pair == 1:
                batch_e.from_core(from_e, grad_e.at[phase])
            if turn == 0 and pair == 3:
                batch_d.second()

        attend_backward(
            lambda pair: qkv_ref[rows, column(pair)],
            lambda pair: qkv_ref[rows, column(pair, width)],
            lambda pair: qkv_ref[rows, column(pair, 2 * width)],
            lambda pair: grad_mixed[:, column(pair)],
            ids_ref[row] == ids_row_ref[row],
            totals_ref.at[row], put(0), put(width), put(2 * width), between,
        )
    shape = (4, 2, 2, each, width)
    grad_mix = mm_tn(mixed_ref[first_rows, :], first_branch) + mm_tn(mixed_ref[rows, :], branch)
    grad_a[:, :, :, 3 * each :, :] = grad_mix.astype(BF16).reshape(shape)
    for part in range(3):
        cols = slice(part * width, (part + 1) * width)
        value = mm_tn(x_ref[...], grad_qkv[:, cols])
        grad_a[:, :, :, part * each : (part + 1) * each, :] = value.astype(BF16).reshape(shape)
    batch_a.start()
    batch_c.second()
    grad_x_ref[...] += mm_nt(grad_qkv[...], qkv_w_ref[...])
    from_v.wait_recv()
    vec_1[0:8, :] = vec_own[...] + vec_core[...]
    vec_1[8:9, :] = first_vectors[0][0] + first_vectors[1][0]
    vec_1[9:10, :] = first_vectors[0][1] + first_vectors[1][1]
    vec_1[10:16, :] = jnp.zeros((6, width), F32)
    vec_x = ex.copy(vec_1, vec_in.at[0], (ex.along_x, phase))

    def put_ff(half):
        def put(rows, value):
            sums[half, rows, :] = value

        return put

    def put_attention(rows, value):
        red_attention_ref[rows, :] = value

    cross_sum = red_cross_ref.at[phase]

    def put_cross_sum(rows, value):
        cross_sum[rows, :] = value

    batch_d.put, batch_e.put, batch_c.put, batch_a.put = put_ff(1), put_ff(0), put_cross_sum, put_attention
    batch_e.second()
    batch_d.third()
    vec_x.wait_recv()
    vec_2[...] = vec_1[...] + vec_in[0]
    vec_y = ex.copy(vec_2, vec_in.at[1], (ex.along_y, phase))
    batch_c.third()
    batch_a.second()
    vec_y.wait_recv()
    vec_3[...] = vec_2[...] + vec_in[1]
    vec_z = [
        ex.copy(vec_3, vec_in.at[2 + j], (index_of(ex.x, ex.y, zz), phase)) for j, zz in enumerate(ex.zs)
    ]
    batch_e.third()
    batch_d.last()
    batch_c.last()
    cross_copy = ex.to_core(cross_sum, red_cross_ref.at[phase])
    batch_a.third()
    batch_e.last()
    ff_copy = ex.to_core(sums.at[1 - phase], red_ff_ref.at[phase])
    red_ff_ref[phase] = sums[phase]
    for copy in vec_z:
        copy.wait_recv()
    vectors_ref[...] = vec_3[...] + vec_in[2] + vec_in[3] + vec_in[4]
    batch_a.last()
    cross_copy.wait_recv()
    ff_copy.wait_recv()
    ex.finish()


def unpack_kernel(ff_ref, attention_ref, cross_halves_ref, qkv_ref, mix_ref, up_ref, down_ref, cq_ref, ckv_ref, co_ref, place_ref):
    width = mix_ref.shape[1]
    high = mix_ref.shape[0]
    for block in range(up_ref.shape[1] // width):
        up_ref[:, block * width : (block + 1) * width] = ff_ref[0, block * high : (block + 1) * high, :]
    down_ref[...] = ff_ref[1]
    for block in range(3):
        qkv_ref[:, block * width : (block + 1) * width] = attention_ref[block * high : (block + 1) * high, :]
    mix_ref[...] = attention_ref[3 * high :, :]
    half_rows = cross_halves_ref.shape[1]

    def cross(start):
        half, row = divmod(start, half_rows)
        return cross_halves_ref[half, row : row + 16, :]

    for start in range(0, 5 * high, 16):
        part, inner = start // high, slice(start % high, start % high + 16)
        if part == 0:
            cq_ref[inner, :] = cross(start)
        elif part < 3:
            ckv_ref[inner, (part - 1) * width : part * width] = cross(start)
        elif part == 3:
            co_ref[inner, :] = cross(start)
        else:
            value = cross(start)
            cols = place_ref.shape[1]
            at = start % high
            place_ref[at : at + 16, :] = value[:, :cols]
            place_ref[high + at : high + at + 16, :] = value[:, cols:]


def whole(shape, dtype):
    return jax.ShapeDtypeStruct(shape, dtype)


def in_vmem(count):
    return [pl.BlockSpec(memory_space=VMEM)] * count


def swap(value):
    return lax.ppermute(value, "phase", [(0, 1), (1, 0)])


def unpacked(shards, height, columns):
    groups, rows, width = shards.shape
    blocks = columns // width
    parts = shards.reshape(groups, blocks, rows // blocks, width)
    return parts.transpose(0, 2, 1, 3).reshape(height, columns)


def token_head(numbers, cap, block_rows, low, flags, labels_all, flags_all, weight, weight_t, scale):
    length, width = low.shape
    dp = lax.axis_size("dp")
    shard = weight_t.shape[0]

    def choice(flags):
        place = jnp.cumsum(flags, axis=-1) - 1
        places = lax.broadcasted_iota(jnp.int32, flags.shape[:-1] + (cap, flags.shape[-1]), flags.ndim - 1)
        return (places == place[..., None, :]) & (flags[..., None, :] > 0)

    chosen = choice(flags)
    packed = mm(chosen.astype(BF16), low).astype(BF16)
    every = gather_blocks(packed, numbers[0]).reshape(2 * dp * cap, width)
    labels = jnp.max(jnp.where(choice(flags_all), labels_all[:, None, :], -1), axis=-1)
    labels = labels.reshape(dp, 2, cap).transpose(1, 0, 2).reshape(2 * dp * cap)
    tall = block_rows
    count = 2 * dp * cap // tall
    probs, totals = pl.pallas_call(
        token_forward,
        grid=(count,),
        out_shape=(whole((count, shard, tall), BF16), whole((count, 1, tall), F32)),
        in_specs=[
            pl.BlockSpec((tall, width), lambda i: (i, 0)),
            pl.BlockSpec((shard, width), lambda i: (0, 0)),
        ],
        out_specs=(
            pl.BlockSpec((1, shard, tall), lambda i: (i, 0, 0)),
            pl.BlockSpec((1, 1, tall), lambda i: (i, 0, 0)),
        ),
        compiler_params=pltpu.CompilerParams(vmem_limit_bytes=48 * 1024 * 1024),
        name="token_forward",
    )(every, weight_t)
    shares = token_shares(totals, numbers[1])
    each = tall // cap
    grad_low, grad_weight = pl.pallas_call(
        partial(token_backward, scale),
        grid=(count,),
        out_shape=(whole((2 * dp, cap, width), BF16), whole((width, shard), F32)),
        in_specs=[
            pl.BlockSpec((1, shard, tall), lambda i: (i, 0, 0)),
            pl.BlockSpec((1, 1, tall), lambda i: (i, 0, 0)),
            pl.BlockSpec((1, 1, tall), lambda i: (i, 0, 0)),
            pl.BlockSpec((tall, width), lambda i: (i, 0)),
            pl.BlockSpec((shard, width), lambda i: (0, 0)),
        ],
        out_specs=(
            pl.BlockSpec((each, cap, width), lambda i: (i, 0, 0)),
            pl.BlockSpec((width, shard), lambda i: (0, 0)),
        ),
        scratch_shapes=[VMEM((shard, width), F32)],
        compiler_params=pltpu.CompilerParams(vmem_limit_bytes=48 * 1024 * 1024),
        name="token_backward",
    )(probs, shares, labels.reshape(count, 1, tall), every, weight_t)
    back = scatter_blocks(grad_low.reshape(2, dp, cap, width), numbers[2])
    return mm_tn(chosen.astype(BF16), back.astype(BF16)), grad_weight


def on_device(
    inputs, segments, delete_target, place_target, token_target, token_mask,
    attention_in, attention_out, feedforward_in, feedforward_out, norm_gain, norm_bias,
    cross_query, cross_keyvalue, cross_out, cross_gain, cross_bias,
    head_delete, head_place, head_token,
):
    phase = lax.axis_index("phase")
    dp_index, dp = lax.axis_index("dp"), lax.axis_size("dp")
    count, length, width = inputs.shape[1:]
    assert count == 2
    hidden = feedforward_in.shape[2]
    scale = float(count * length * dp) ** (-0.5)
    any_space = pl.BlockSpec(memory_space=pl.ANY)
    params = pltpu.CompilerParams(vmem_limit_bytes=56 * 1024 * 1024)

    coded = jnp.where(token_mask == 1, token_target, -1)
    labels_all = lax.all_gather(coded, "dp", tiled=True)
    flags_all = (labels_all >= 0).astype(jnp.int32)

    def row_of(value):
        return lax.dynamic_index_in_dim(value, phase, 0, keepdims=False)

    own_norms = jnp.stack([norm_gain[0, 1], norm_bias[0, 1]])
    up_other, down_other = swap(feedforward_in[0]), swap(feedforward_out[0])
    other_norms = swap(own_norms)
    is_enc = phase == 0
    norms = jnp.concatenate(
        [jnp.where(is_enc, own_norms, other_norms), jnp.where(is_enc, other_norms, own_norms)]
    )
    ids = row_of(segments)
    own_ids = lax.dynamic_index_in_dim(segments, phase, 1, keepdims=False)
    states = inputs[0].reshape(count * length, width)

    qkv, mixed, res, totals, keep, send = pl.pallas_call(
        self_forward,
        out_shape=(
            whole((count * length, 3 * width), BF16),
            whole((count * length, width), BF16),
            whole((count * length, width), F32),
            whole((count, HEADS, length), F32),
            whole((length, width), F32),
            whole((length, width), F32),
        ),
        in_specs=in_vmem(7),
        out_specs=tuple(in_vmem(6)),
        compiler_params=params,
        name="self_forward",
    )(states, own_ids[:, :, None], own_ids[:, None, :], attention_in[0], attention_out[0], norm_gain[0], norm_bias[0])
    received = swap(send)

    ids_e, ids_d_row = ids[0][:, None], ids[1][None, :]
    pair_valid = jnp.concatenate([ids[1, :-1] == ids[1, 1:], jnp.zeros((1,), bool)])
    targets = jnp.stack(
        [row_of(delete_target), row_of(place_target), pair_valid.astype(jnp.int32)], axis=1
    )
    delete_weight = jnp.pad(head_delete, ((0, 0), (0, 126)))
    gain_row, bias_row = cross_gain[None, :], cross_bias[None, :]
    ff_scratch = [
        VMEM((width, hidden), BF16), VMEM((hidden, width), BF16),
        VMEM((width, hidden), BF16), VMEM((hidden, width), BF16),
    ]
    saved_shapes = (
        whole((length, width), F32),
        whole((length, width), F32),
        whole((length, width), F32),
        whole((length, 2 * width), BF16),
        whole((length, width), BF16),
        whole((length, width), BF16),
        whole((length, width), F32),
        whole((HEADS, length), F32),
        whole((length, hidden), BF16), whole((length, hidden), BF16),
        whole((length, hidden), BF16), whole((length, hidden), BF16),
        whole((length, width), F32),
        whole((length, width), BF16),
    )
    classes = head_place.shape[1]
    each = width // GROUPS
    outs = pl.pallas_call(
        partial(rows_forward, scale),
        out_shape=saved_shapes + (
            whole((length, width), BF16),
            whole((length, width), F32),
            whole((8, width), F32),
            whole((GROUPS, each, 2 * classes), BF16),
        ),
        in_specs=in_vmem(5) + [any_space] * 4 + in_vmem(8),
        out_specs=tuple(in_vmem(18)),
        scratch_shapes=ff_scratch + [pltpu.SemaphoreType.DMA((2, 2))],
        compiler_params=params,
        name="rows_forward",
    )(
        keep, received, ids_e, ids_d_row, targets,
        feedforward_in[0], up_other, feedforward_out[0], down_other, norms,
        cross_query, cross_keyvalue, cross_out, gain_row, bias_row, delete_weight, head_place,
    )
    saved = outs[:14]
    low, grad_low, grad_delete, grad_place = outs[14:]

    shard = head_token.shape[1] // (2 * dp)
    weight = lax.dynamic_slice_in_dim(head_token, (dp_index * 2 + phase) * shard, shard, 1)
    weight_t = weight.T
    flags = row_of(token_mask)

    def run_head(numbers, cap, block_rows):
        return token_head(numbers, cap, block_rows, low, flags, labels_all, flags_all, weight, weight_t, scale)

    small = length // 2
    fits = jnp.max(jnp.sum(flags_all, axis=1)) <= small
    grad_token, grad_weight = lax.cond(
        fits, lambda: run_head((1, 2, 3), small, 4 * small), lambda: run_head((4, 5, 6), length, 2 * length)
    )
    other_weight = swap(grad_weight)
    grad_head_token = jnp.concatenate(
        [jnp.where(is_enc, grad_weight, other_weight), jnp.where(is_enc, other_weight, grad_weight)], axis=1
    )

    each = width // GROUPS
    ff_rows = 2 * hidden // GROUPS
    if dp == GROUPS:
        half_rows = 5 * each // 2
        ff_half, attention_rows = ff_rows // 2, 4 * each
        rows_of = (ff_half, ff_half, half_rows, attention_rows)

        def shards(rows, *lead):
            return VMEM(lead + (rows, width), BF16)

        grad_states, red_ff, red_attention, red_cross, vectors = pl.pallas_call(
            backward_kernel,
            out_shape=(
                whole((count * length, width), F32), whole((2, ff_half, width), F32),
                whole((attention_rows, width), F32), whole((2, half_rows, width), F32), whole((16, width), F32),
            ),
            in_specs=in_vmem(4) + [any_space] * 4 + in_vmem(6 + 8) + [any_space] * 4 + in_vmem(14),
            out_specs=tuple(in_vmem(5)),
            scratch_shapes=[
                VMEM((width, hidden), BF16), VMEM((hidden, width), BF16),
                VMEM((length, hidden), BF16), VMEM((length, hidden), BF16),
                shards(ff_half, 2, 4, 2, 2), shards(ff_half, 2, 4, 2, 2), shards(half_rows, 2, 4, 2, 2),
                shards(attention_rows, 4, 2, 2),
                shards(ff_half, 4, 2, 2), shards(ff_half, 4, 2, 2), shards(half_rows, 4, 2, 2),
                *[shards(rows, 4, 2) for rows in rows_of],
                *[shards(rows, 4) for rows in rows_of],
                *[shards(rows, 3) for rows in rows_of],
                VMEM((2, length, width), F32), VMEM((length, width), F32),
                VMEM((length, width), BF16), VMEM((length, 2 * width), BF16), VMEM((count * length, 3 * width), BF16),
                VMEM((2, ff_half, width), F32),
                VMEM((8, width), F32), VMEM((8, width), F32),
                VMEM((16, width), F32), VMEM((16, width), F32), VMEM((16, width), F32), VMEM((5, 16, width), F32),
                pltpu.SemaphoreType.DMA((8,)), pltpu.SemaphoreType.DMA((56,)), pltpu.SemaphoreType.DMA((56,)),
            ],
            compiler_params=pltpu.CompilerParams(
                collective_id=0, has_side_effects=True, vmem_limit_bytes=60 * 1024 * 1024
            ),
            name="backward",
        )(
            grad_low, grad_token, ids_e, ids_d_row,
            feedforward_in[0], up_other, feedforward_out[0], down_other, norms,
            cross_query, cross_keyvalue, cross_out, gain_row, bias_row, *saved, grad_place, grad_delete,
            states, own_ids[:, :, None], own_ids[:, None, :], attention_in[0], attention_out[0], norm_gain[0],
            qkv, mixed, res, totals,
        )
        grads = pl.pallas_call(
            unpack_kernel,
            out_shape=(
                whole((each, 3 * width), F32), whole((each, width), F32), whole((each, hidden), F32),
                whole((hidden // GROUPS, width), F32), whole((each, width), F32), whole((each, 2 * width), F32),
                whole((each, width), F32), whole((2 * each, classes), F32),
            ),
            in_specs=in_vmem(3),
            out_specs=tuple(in_vmem(8)),
            compiler_params=params,
            name="unpack",
        )(red_ff, red_attention, red_cross)
        g_qkv, g_mix, g_up, g_down, g_cq, g_ckv, g_co, g_place = grads
        vectors = lax.dynamic_slice_in_dim(vectors, dp_index * each, each, 1)
        second = jnp.where(is_enc, vectors[0:2], vectors[2:4])
        vector_out = jnp.concatenate([vectors[8:9], second[0:1], vectors[9:10], second[1:2], vectors[4:8]])
    else:
        keep, send, ff_own, ff_other, cross_shards, vectors = pl.pallas_call(
            rows_backward,
            out_shape=(
                whole((length, width), F32), whole((length, width), F32),
                whole((GROUPS, ff_rows, width), BF16), whole((GROUPS, ff_rows, width), BF16),
                whole((GROUPS, 5 * each, width), BF16), whole((8, width), F32),
            ),
            in_specs=in_vmem(4) + [any_space] * 4 + in_vmem(6 + 14 + 1),
            out_specs=(in_vmem(2) + [any_space] * 2 + in_vmem(2)),
            scratch_shapes=ff_scratch + [
                VMEM((GROUPS, ff_rows, width), BF16), VMEM((GROUPS, ff_rows, width), BF16),
                VMEM((length, width), F32), VMEM((length, width), F32),
                VMEM((length, width), BF16), VMEM((length, 2 * width), BF16),
                pltpu.SemaphoreType.DMA((2, 2)), pltpu.SemaphoreType.DMA((2,)),
            ],
            compiler_params=params,
            name="rows_backward",
        )(
            grad_low, grad_token, ids_e, ids_d_row,
            feedforward_in[0], up_other, feedforward_out[0], down_other, norms,
            cross_query, cross_keyvalue, cross_out, gain_row, bias_row, *saved, grad_place,
        )
        received = swap(send)
        ff_received = swap(ff_other)
        half_rows = 5 * each // 2
        cross_keep = lax.dynamic_slice_in_dim(cross_shards, phase * half_rows, half_rows, 1)
        cross_received = swap(lax.dynamic_slice_in_dim(cross_shards, (1 - phase) * half_rows, half_rows, 1))
        shared = jnp.concatenate([vectors[4:6], grad_delete[:2]])
        norm_own = jnp.where(is_enc, vectors[0:2], vectors[2:4])
        norm_other = jnp.where(is_enc, vectors[2:4], vectors[0:2])
        vector_received = swap(jnp.concatenate([norm_other, shared]))
        vector_sums = jnp.concatenate([norm_own, shared]) + vector_received

        grad_states, attention_shards, first_vectors = pl.pallas_call(
            self_backward,
            out_shape=(
                whole((count * length, width), F32), whole((GROUPS, 4 * each, width), BF16), whole((8, width), F32),
            ),
            in_specs=in_vmem(12),
            out_specs=tuple(in_vmem(3)),
            scratch_shapes=[VMEM((count * length, width), F32), VMEM((count * length, 3 * width), BF16)],
            compiler_params=params,
            name="self_backward",
        )(
            keep, received, states, own_ids[:, :, None], own_ids[:, None, :], attention_in[0], attention_out[0],
            norm_gain[0], qkv, mixed, res, totals,
        )

        all_vectors = jnp.stack([
            first_vectors[0], vector_sums[0], first_vectors[1], vector_sums[1],
            vector_sums[2], vector_sums[3], vector_sums[4], vector_sums[5],
        ])
        ff_sum = (ff_own.astype(F32) + ff_received.astype(F32)).astype(BF16)
        cross_sum = (cross_keep.astype(F32) + cross_received.astype(F32)).astype(BF16)
        cross_other = swap(cross_sum)
        cross_all = jnp.concatenate(
            [jnp.where(is_enc, cross_sum, cross_other), jnp.where(is_enc, cross_other, cross_sum)], axis=1
        )
        ff_up = hidden // width * each

        def spread(value):
            return lax.psum_scatter(value.astype(F32), "dp", scatter_dimension=0, tiled=True)

        g_qkv = spread(unpacked(attention_shards[:, : 3 * each], width, 3 * width))
        g_mix = spread(unpacked(attention_shards[:, 3 * each :], width, width))
        g_up = spread(unpacked(ff_sum[:, :ff_up], width, hidden))
        g_down = spread(unpacked(ff_sum[:, ff_up:], hidden, width))
        g_cq = spread(unpacked(cross_all[:, :each], width, width))
        g_ckv = spread(unpacked(cross_all[:, each : 3 * each], width, 2 * width))
        g_co = spread(unpacked(cross_all[:, 3 * each : 4 * each], width, width))
        place = cross_all[:, 4 * each :].reshape(GROUPS, each, 2, classes)
        g_place = spread(place.transpose(0, 2, 1, 3).reshape(2 * width, classes))
        vector_out = lax.psum_scatter(all_vectors, "dp", scatter_dimension=1, tiled=True)
    return (
        grad_states.reshape(1, count, length, width),
        g_qkv[None], g_mix[None], g_up[None], g_down[None],
        vector_out[None, 0:2], vector_out[None, 2:4],
        g_cq, g_ckv, g_co, vector_out[4], vector_out[5], vector_out[6:8].T, g_place, grad_head_token,
    )


def solution(mesh):
    layer, row = P("phase", None, None), P("dp", None)
    return jax.shard_map(
        on_device,
        mesh=mesh,
        in_specs=(P("phase", "dp", None, None), P("dp", None, None), row, row, row, row)
        + (layer,) * 6 + (P(),) * 8,
        out_specs=(P("phase", "dp", None, None),) + (P("phase", "dp", None),) * 4
        + (P("phase", None, "dp"),) * 2 + (row,) * 3 + (P("dp"),) * 2 + (row,) * 2 + (P(None, "dp"),),
        check_vma=False,
    )
```

time: 3070 us -> 318 us (0.10)
  waiting for transfers between devices: 2220 us -> 0.01 us
  starting transfers between devices: 334 us -> 1.27 us
  Pallas kernels: 0 us -> 226 us
  other arithmetic: 158 us -> 12.3 us
  local copies, waits for them, and re-layouts: 162 us -> 18.6 us
  matrix products: 105 us -> 1.12 us
    reduce_scatter x9 -> x0, waiting for transfers between devices: 2060 us -> none  [the longest x1 1360 us: on_device(): lax.psum_scatter(token_sum, 'dp', scatter_dimension=1, tiled=True)]
    ppermute x3 -> x5, starting transfers between devices: 329 us -> 1.27 us  [swap(): return lax.ppermute(value, 'phase', [(0, 1), (1, 0)])]
    pallas_call x0 -> x9, Pallas kernels: none -> 226 us  [the longest x1 107 us: on_device(): pl.pallas_call(backward_kernel, out_shape=(whole((count * length, width),...]
    unnamed x17 -> x0, waiting for transfers between devices: 118 us -> none
    add x15 -> x0, other arithmetic: 101 us -> none  [the longest x1 83.7 us: on_device(): token_sum = token_sum + validity * token_piece]
    dot_general x66 -> x2, matrix products: 95.8 us -> 1.12 us  [the longest x1 0.85 us: mm(): return jnp.dot(left, right, preferred_element_type=F32)]
    another operation x41 -> x9, local copies, waits for them, and re-layouts: 88 us -> 3.4 us  [the longest x2 1.5 us: on_device(): jnp.stack([row_of(delete_target), row_of(place_target), pair_valid.astype...]
    unnamed x1 -> x0, blocking collectives: 42.9 us -> none
  transfers between devices with their start and end apart: 17 -> 5, of which waited for: 16 -> 0; matrix products, arithmetic and copies ran while one was open for 8% -> 5% of each run, Pallas kernels for 0% -> 35%
where the time goes in v1:
time: 318 us; the launch traced here: 312 us
  Pallas kernels  226 us (71%)
  blocking collectives  42.5 us (13%)
  local copies, waits for them, and re-layouts  18.6 us (6%)
  other arithmetic  12.3 us (4%)
  loops' own time  8.88 us (3%)
    pallas_call x1, Pallas kernels, on_device(): pl.pallas_call(backward_kernel, out_shape=(whole((count * length, width),...  107 us
    all_gather x1, blocking collectives, on_device(): labels_all = lax.all_gather(coded, 'dp', tiled=True)  42.5 us
    pallas_call x1, Pallas kernels, scatter_blocks(): pl.pallas_call(scatter_kernel, out_shape=jax.ShapeDtypeStruct((rows, widt...  28.6 us
    pallas_call x1, Pallas kernels, gather_blocks(): pl.pallas_call(gather_kernel, out_shape=jax.ShapeDtypeStruct((2, 4, 2, 2,...  24.2 us
    pallas_call x1, Pallas kernels, token_head(): pl.pallas_call(partial(token_backward, scale), grid=(count,), out_shape=(...  15.6 us
    pallas_call x1, Pallas kernels, on_device(): pl.pallas_call(partial(rows_forward, scale), out_shape=saved_shapes + (wh...  15 us
    pallas_call x1, Pallas kernels, token_shares(): pl.pallas_call(share_kernel, out_shape=jax.ShapeDtypeStruct((rows, 128),...  13.1 us
    pallas_call x1, Pallas kernels, token_head(): pl.pallas_call(token_forward, grid=(count,), out_shape=(whole((count, sha...  11.9 us
  transfers between devices with their start and end apart: 5, of which 0 were waited for; matrix products, arithmetic and copies ran while one was open for 5% of the time, Pallas kernels for 35%

profile of v1, /device:TPU:0, one launch (start us, length us, event | category | flops | bytes accessed | tf_op | source)
XLA Modules:
  0.0 312.5 jit_solution(328098992580678087)
XLA Ops:
  0.7 1.3 fusion.28
  2.0 0.8 broadcast_in_dim.78.ids_ref
  2.8 8.8 %self_forward.1 = (bf16[512,1536]{1,0:T(8,128)(2,1)}, bf16[512,512]{1,0:T(8,128)(2,1)}, f32[512,512]{1,0:T(8,128)}, f32[2,8,256]{2,1,0:T(8,128)}, f32[256,512]{1,0:T(8,128)}, /*index=5*/f32[256,512]{1,0:T(8,128)}) custom-call(bf16[512,512]{1,0:T(8,128)(2,1)} %bitcast.106, s32[2,256,1]{2,1,0:T(8,128)} %broadcast_in_dim.78.ids_ref, ...), custom_call_target="tpu_custom_call" | custom-call | tf_op jit(solution)/shard_map/self_forward/pallas_call | solution.py:1238
  11.6 0.5 collective-permute-start
  12.1 0.5 collective-permute-start.2
  12.6 0.7 slice_bitcast_fusion
  13.3 0.1 collective-permute-start.3
  13.4 0.7 fusion.21
  14.1 42.5 %all-gather = s32[16,2,256]{2,1,0:T(2,128)S(1)} all-gather(s32[1,2,256]{2,1,0:T(2,128)S(1)} %fusion.21), channel_id=1, replica_groups=mesh['dp'=16,'phase'=2] {'dp'}, dimensions={0}, use_global_device_ids=true | all-gather | bytes 34816 | tf_op jit(solution)/shard_map/all_gather | solution.py:1221
  56.7 0.7 fusion.20
  57.5 0.7 fusion.22
  58.3 2.3 constant_dynamic-slice_fusion.3
  60.6 0.6 fusion.25
  61.2 0.8 copy.76.targets_ref
  62.0 0.8 copy.75.ids_e_ref
  62.8 0.2 copy.74
  63.0 1.5 copy.80
  64.5 0.6 reduce_max.27
  65.8 0.7 pad.4.delete_w_ref
  66.5 0.6 pad_maximum_fusion.1.norms_ref
  67.1 1.3 copy-done.5
  68.4 15.0 %rows_forward.1 = (f32[256,512]{1,0:T(8,128)}, f32[256,512]{1,0:T(8,128)}, f32[256,512]{1,0:T(8,128)}, bf16[256,1024]{1,0:T(8,128)(2,1)}, bf16[256,512]{1,0:T(8,...) custom-call(f32[256,512]{1,0:T(8,128)} %get-tuple-element.92.keep_re, ...), custom_call_target="tpu_custom_call" | custom-call | tf_op jit(solution)/shard_map/rows_forward/pallas_call | solution.py:1282
  83.5 109.6 %conditional.1 = (f32[256,512]{1,0:T(8,128)S(1)}, f32[512,1024]{1,0:T(8,128)}) conditional(s32[]{:T(128)} %convert_element_type.36, (s32[256]{0:T(256)S(1)}, bf16[256,512]{1,0:T(8,128)(2,1)S(1)}, bf16[1024,512]{1,0:T(8,128)(2,1)S(1)}, s32[32,256]{1,0:T(8,128)S(1)}, s32[32,256]{1,0:T(8,128)S(1)}) %tuple.35, (s32[256]{0:T(256)S(1)}, ...), branch_computations={%region_2.8_spmd, %region_8.14_spmd} | conditional | flops 144220768 | bytes 18458416 | solution.py:1313
  92.3 0.3 reduce-window.28
  92.7 0.1 slice_reduce_fusion.3
  92.9 0.9 convolution_convert_fusion.1.block_ref
  93.8 24.2 %gather_blocks.3 = bf16[2,4,2,2,128,512]{5,4,3,2,1,0:T(8,128)(2,1)} custom-call(bf16[128,512]{1,0:T(8,128)(2,1)} %convolution_convert_fusion.1.block_ref), custom_call_target="tpu_custom_call" | custom-call | tf_op jit(solution)/shard_map/cond/branch_1_fun/gather_blocks/pallas_call | solution.py:592
  118.0 2.2 copy-done
  120.2 11.9 %token_forward.3 = (bf16[8,1024,512]{2,1,0:T(8,128)(2,1)}, f32[8,1,512]{2,1,0:T(1,128)S(1)}) custom-call(bf16[4096,512]{1,0:T(8,128)(2,1)S(1)} %bitcast.86, bf16[1024,512]{1,0:T(8,128)(2,1)S(1)} %get-tuple-element.31.weight_ref), custom_call_target="tpu_custom_call" | custom-call | tf_op jit(solution)/shard_map/cond/branch_1_fun/token_forward/pallas_call | solution.py:1165
  132.1 0.6 copy-done.4
  132.7 13.1 %token_shares.3 = f32[32,128]{1,0:T(8,128)} custom-call(f32[32,128]{1,0:T(8,128)} %bitcast.92), custom_call_target="tpu_custom_call" | custom-call | tf_op jit(solution)/shard_map/cond/branch_1_fun/token_shares/pallas_call | solution.py:739
  145.8 0.6 reduce-window.30
  146.4 0.2 slice_reduce_fusion.2
  146.8 1.1 select_reduce_fusion.1
  147.8 0.7 copy-done.2
  148.5 15.6 %token_backward.3 = (bf16[32,128,512]{2,1,0:T(8,128)(2,1)S(1)}, f32[512,1024]{1,0:T(8,128)}) custom-call(bf16[8,1024,512]{2,1,0:T(8,128)(2,1)} %get-tuple-element.32.probs_ref, f32[8,1,512]{2,1,0:T(1,128)S(1)} %bitcast.89, s32[8,1,512]{2,1,0:T(1,128)S(1)} %bitcast.90, bf16[4096,512]{1,0:T(8,128)(2,1)} %bitcast.85, ...), custom_call_target="tpu_custom_call" | custom-call | tf_op jit(solution)/shard_map/cond/branch_1_fun/token_backward/pallas_call | solution.py:1182
  164.2 28.6 %scatter_blocks.3 = f32[128,512]{1,0:T(8,128)S(1)} custom-call(bf16[2,4,2,2,128,512]{5,4,3,2,1,0:T(8,128)(2,1)S(1)} %bitcast.87), custom_call_target="tpu_custom_call" | custom-call | tf_op jit(solution)/shard_map/cond/branch_1_fun/scatter_blocks/pallas_call | solution.py:682
  192.8 0.3 fusion.11
  193.1 0.2 collective-permute-start.4
  193.2 106.7 %backward.1 = (f32[512,512]{1,0:T(8,128)}, f32[2,128,512]{2,1,0:T(8,128)}, f32[128,512]{1,0:T(8,128)}, f32[2,80,512]{2,1,0:T(8,128)}, f32[16,512]{1,0:T(8,128)}) custom-call(f32[256,512]{1,0:T(8,128)} %get-tuple-element.94.grad_low_ref, f32[256,512]{1,0:T(8,128)S(1)} %get-tuple-element.96.grad_token_ref, s32[256,1]{1,0:T(8,128)} %copy.75.ids_e_ref, ...), custom_call_target="tpu_custom_call" | custom-call | tf_op jit(solution)/shard_map/backward/pallas_call | solution.py:1331
  300.0 2.2 unpack.1
  302.2 1.3 dynamic-slice_bitcast_fusion.1
  303.5 1.4 dynamic-slice_bitcast_fusion
  304.9 0.6 maximum_bitcast_fusion.1
  305.5 0.6 maximum_bitcast_fusion
  306.1 2.7 broadcast_select_fusion.1
  308.8 2.5 pad_maximum_fusion
  311.3 1.0 copy.94
  (38 shorter events, 0.8 us)
Async XLA Ops:
  0.6 60.0 %copy-start.7 = (s32[2,2,256]{2,1,0:T(2,128)S(1)}, s32[2,2,256]{2,1,0:T(2,128)}, u32[]{:S(2)}) copy-start(s32[2,2,256]{2,1,0:T(2,128)} %param.23) | copy-start | bytes 12292
  0.7 60.5 %copy-start.8 = (s32[2,256]{1,0:T(2,128)S(1)}, s32[2,256]{1,0:T(2,128)}, u32[]{:S(2)}) copy-start(s32[2,256]{1,0:T(2,128)} %param.27) | copy-start | bytes 6148
  0.7 62.1 %copy-start.9 = (bf16[512,2]{0,1:T(2,128)(2,1)S(1)}, bf16[512,2]{0,1:T(2,128)(2,1)}, u32[]{:S(2)}) copy-start(bf16[512,2]{0,1:T(2,128)(2,1)} %param.39) | copy-start | bytes 6148
  11.6 55.5 %collective-permute-start = (f32[256,512]{1,0:T(8,128)}, f32[256,512]{1,0:T(8,128)}, u32[]{:S(2)}, u32[]{:S(2)}) collective-permute-start(f32[256,512]{1,0:T(8,128)} %get-tuple-element.93), channel_id=1, source_target_pairs={{0,1},{1,0},{2,3},{3,2},{4,5},{5,4},{6,7},{7,6},{8,9},{9,8},{10,11... | collective-permute-start | bytes 1572872 | tf_op jit(solution)/shard_map/ppermute | solution.py:1138
  12.1 55.0 %collective-permute-start.1 = (bf16[512,2048]{1,0:T(8,128)(2,1)}, bf16[512,2048]{1,0:T(8,128)(2,1)S(1)}, u32[]{:S(2)}, u32[]{:S(2)}) collective-permute-start(bf16[512,2048]{1,0:T(8,128)(2,1)} %bitcast.98), channel_id=1, source_target_pairs={{0,1},{1,0},{2,3},{3,2},{4,5},{5,4},{6,7},{7,6},{8,9},{9,8},{10,11... | collective-permute-start | bytes 6291464 | tf_op jit(solution)/shard_map/ppermute | solution.py:1138
  12.1 55.0 %collective-permute-start.2 = (bf16[2048,512]{1,0:T(8,128)(2,1)}, bf16[2048,512]{1,0:T(8,128)(2,1)}, u32[]{:S(2)}, u32[]{:S(2)}) collective-permute-start(bf16[2048,512]{1,0:T(8,128)(2,1)} %bitcast.101), channel_id=1, source_target_pairs={{0,1},{1,0},{2,3},{3,2},{4,5},{5,4},{6,7},{7,6},{8,9},{9,8},{10,11... | collective-permute-start | bytes 6291464 | tf_op jit(solution)/shard_map/ppermute | solution.py:1138
  13.3 53.2 %collective-permute-start.3 = (f32[2,512]{1,0:T(2,128)S(1)}, f32[2,512]{1,0:T(2,128)S(1)}, u32[]{:S(2)}, u32[]{:S(2)}) collective-permute-start(f32[2,512]{1,0:T(2,128)S(1)} %pad_maximum_fusion.2), channel_id=1, source_target_pairs={{0,1},{1,0},{2,3},{3,2},{4,5},{5,4},{6,7},{7,6},{8,9},{9,8},{10,11... | collective-permute-start | bytes 12296 | tf_op jit(solution)/shard_map/ppermute | solution.py:1138
  67.1 1.3 copy-start.5
  118.0 2.2 copy-start
  132.1 0.6 copy-start.4
  147.8 0.7 copy-start.2
  193.1 113.0 %collective-permute-start.4 = (f32[512,1024]{1,0:T(8,128)}, f32[512,1024]{1,0:T(8,128)}, u32[]{:S(2)}, u32[]{:S(2)}) collective-permute-start(f32[512,1024]{1,0:T(8,128)} %get-tuple-element.130), channel_id=1, source_target_pairs={{0,1},{1,0},{2,3},{3,2},{4,5},{5,4},{6,7},{7,6},{8,9},{9,8},{10,11... | collective-permute-start | bytes 6291464 | tf_op jit(solution)/shard_map/ppermute | solution.py:1138
  308.8 2.5 copy-start.6
